TPU v7x, 512 devices: a whole 4x4x16 slice. The times are simulated.
512 devices in a mesh: tx: 16 (over z), ty: 32 (over y, x, core).
Axes of the slice: x: 4, y: 4, z: 16, core: 2. Of those that a mesh axis runs over, the one named last changes fastest.
Arguments:
- embedding: float32 [50, 16, 32, 512], P(None, 'tx', 'ty'), may hold values from -8 to 8
- neighbors: int32 [15, 16, 32, 512], P(None, 'tx', 'ty'), may hold values from 0 to 1663, as said below
- slide_id: int32 [16, 32, 512], P('tx', 'ty'), may hold values from 0 to 39, as said below
- live_count: int32 [16, 32], P('tx', 'ty'), may hold values from 128 to 512, as said below
- centroids: float32 [100, 50], replicated, may hold values from -6 to 6
Outputs:
- corrected: float32 [50, 16, 32, 512], P(None, 'tx', 'ty')
- centers: float32 [100, 50], replicated
Inputs may be any that keep to these rules, and one draw needn't show every extreme that they name: `neighbors`: each id names a live cell, either of the cell's own tile or of one of the up to eight bordering tiles inside the grid; an id in a bordering tile names one of that tile's first 128 cells. `slide_id`: the cell slots of one tile, live or not, carry at most 4 distinct slides. The live cells of a tile are its first live_count slots; some tile is full in every draw.
All inputs are finite; a program needn't handle non-finite values.
Results may differ from a plain program's by a relative error of at most 0.0003.
Values sent between devices are 32-bit elements; how exact they have to be, the bound alone decides.
A program may use at most 64 MiB of HBM per device.

v0:
```python
import jax
import jax.numpy as jnp
from jax import lax
from jax.sharding import PartitionSpec as P

SLIDES = 40
SLOTS = 4
ITERS = 2


HIGH = lax.Precision.HIGHEST
SHARPNESS = 20.0


def extended(block, sides, width):
    for axis, dim in sides:
        count = lax.axis_size(axis)
        forward = [(i, i + 1) for i in range(count - 1)]
        backward = [(target, source) for source, target in forward]
        low = lax.ppermute(
            lax.slice_in_dim(block, block.shape[dim] - width, None, axis=dim), axis, forward
        )
        high = lax.ppermute(lax.slice_in_dim(block, 0, width, axis=dim), axis, backward)
        block = jnp.concatenate([low, block, high], axis=dim)
    return block


def unit_columns(values):
    return values / jnp.sqrt(jnp.sum(values * values, axis=0, keepdims=True) + 1.0)


def unit_rows(values):
    return values / jnp.sqrt(jnp.sum(values * values, axis=1, keepdims=True) + 1.0)


def layout(slides, alive, count):
    cells = slides.shape[0]
    ident = lax.broadcasted_iota(jnp.int32, (count, cells), 0)
    same = slides[None, :] == ident
    member = same & alive[None, :]
    present = jnp.any(member, axis=1).astype(jnp.int32)
    rank = jnp.cumsum(present) - present
    cell_rank = jnp.sum(jnp.where(same, rank[:, None], 0), axis=0)
    slot_ids = lax.broadcasted_iota(jnp.int32, (SLOTS, 1), 0)
    livef = alive.astype(jnp.float32)
    masks = (cell_rank[None, :] == slot_ids).astype(jnp.float32) * livef[None, :]
    place = ((rank[None, :] == slot_ids) & (present[None, :] > 0)).astype(jnp.float32)
    return (same.astype(jnp.float32), member.astype(jnp.float32), masks, place, livef)


def per_device(embedding, neighbors, slide_id, live_count, centroids):
    pcs = embedding.shape[0]
    cells = embedding.shape[3]
    bound_cells = cells // 4
    own = embedding.reshape(pcs, cells)
    block = extended(embedding, (("tx", 1), ("ty", 2)), 1)
    width = block.shape[3]
    source = jnp.concatenate([own, block.reshape(pcs, 9 * width)], axis=1)
    ids = neighbors.reshape(neighbors.shape[0], cells)
    outer = ids >= cells
    rel = jnp.maximum(ids - cells, 0)
    direction = rel // bound_cells
    spot = rel - direction * bound_cells
    position = jnp.where(outer, cells + direction * width + spot, ids)
    total = own
    for step in range(ids.shape[0]):
        total = total + jnp.take(source, position[step], axis=1)
    alive = lax.broadcasted_iota(jnp.int32, (cells,), 0) < live_count[0, 0]
    slides = slide_id.reshape(cells)
    same, member, masks, place, livef = layout(slides, alive, SLIDES)
    field = total / (ids.shape[0] + 1.0) * livef[None, :]
    slide_totals = lax.psum(jnp.sum(member, axis=1), ("tx", "ty"))
    centre = centroids
    for turn in range(ITERS):
        unit_y = unit_rows(centre)
        unit_z = unit_columns(field)
        raw = jnp.exp(SHARPNESS * (jnp.dot(unit_y, unit_z, precision=HIGH) - 1.0))
        first = raw / jnp.sum(raw, axis=0, keepdims=True) * livef[None, :]
        occupied = lax.psum(jnp.dot(first, member.T, precision=HIGH), ("tx", "ty"))
        expected = (
            jnp.sum(occupied, axis=1, keepdims=True) * slide_totals[None, :] / jnp.sum(slide_totals)
        )
        ratio = ((expected + 1.0) / (occupied + 1.0)) ** 2
        weighted = raw * jnp.dot(ratio, same, precision=HIGH)
        assign = weighted / jnp.sum(weighted, axis=0, keepdims=True) * livef[None, :]
        slot_sums = jnp.stack(
            [
                jnp.dot(assign * masks[slot][None, :], field.T, precision=HIGH)
                for slot in range(SLOTS)
            ]
        )
        counts_part = jnp.dot(assign, member.T, precision=HIGH)
        sums_part = jnp.einsum("sb,skd->kbd", place, slot_sums, precision=HIGH)
        centre_part = jnp.dot(assign, unit_z.T, precision=HIGH)
        counts, sums, centre_sums = lax.psum((counts_part, sums_part, centre_part), ("tx", "ty"))
        scale = 1.0 / (counts + 1.0)
        mean = jnp.sum(sums * scale[:, :, None], axis=1) / jnp.sum(counts * scale, axis=1)[:, None]
        beta = (sums - counts[:, :, None] * mean[:, None, :]) * scale[:, :, None]
        slot_beta = jnp.einsum("sb,kbd->skd", place, beta, precision=HIGH)
        shift = jnp.zeros_like(field)
        for slot in range(SLOTS):
            shift = (
                shift + jnp.dot(slot_beta[slot].T, assign, precision=HIGH) * masks[slot][None, :]
            )
        field = field - shift
        centre = centre_sums
    return (field.reshape(pcs, 1, 1, cells), unit_rows(centre))


def solution(mesh):
    placed = (
        P(None, "tx", "ty", None),
        P(None, "tx", "ty", None),
        P("tx", "ty", None),
        P("tx", "ty"),
        P(),
    )
    return jax.shard_map(
        per_device,
        mesh=mesh,
        in_specs=placed,
        out_specs=(P(None, "tx", "ty", None), P()),
        check_vma=False,
    )
```

profile of v0, /device:TPU:1, one launch (start us, length us, event | category | flops | bytes accessed | tf_op | source)
XLA Modules:
  0.0 1228.7 jit_solution(13206006863601633927)
XLA Ops:
  7.2 4.4 collective-permute-start
  11.6 1.3 collective-permute-start.1
  12.9 0.9 copy.170
  13.8 0.8 compare_select_fusion
  16.6 0.8 fusion.63
  17.4 1.4 convert_reduce_fusion
  19.1 0.8 select_reduce_fusion
  21.4 0.9 constant_dynamic-update-slice_fusion.1
  22.3 5.7 collective-permute-start.3
  28.1 1.9 collective-permute-start.2
  30.8 2.9 collective-permute-done.2
  33.8 0.8 pad_maximum_fusion
  35.3 1.1 pad_maximum_fusion.1
  36.3 1.9 copy.83
  38.3 1.0 gather_fusion.14
  39.4 1.0 gather_fusion.13
  40.6 1.0 gather_fusion.12
  41.8 1.0 gather_fusion.11
  43.0 1.0 gather_fusion.10
  44.8 1.0 gather_fusion.9
  46.6 1.0 gather_fusion.8
  48.4 1.0 gather_fusion.7
  50.2 1.0 gather_fusion.6
  51.2 0.8 copy.96
  52.0 1.0 gather_fusion.5
  53.8 1.0 gather_fusion.4
  55.6 1.0 gather_fusion.3
  57.4 1.0 gather_fusion.2
  58.5 0.8 copy.88
  59.3 1.0 gather_fusion.1
  60.3 0.8 copy.86
  61.1 1.0 gather_fusion
  62.3 1.5 multiply_reduce_fusion.3
  63.8 1.0 fusion.133
  65.2 112.0 %all-reduce.2 = (f32[100,40]{0,1:T(8,128)S(1)}, f32[40]{0:T(128)S(1)}) all-reduce(f32[100,40]{0,1:T(8,128)S(1)} %fusion.38, f32[40]{0:T(128)} %convert_reduce_fusion), channel_id=1, replica_groups=mesh['tx'=16,'ty'=32] {'tx','ty'}, use_global_device_ids=true, to_apply=%region_5.7 | all-reduce | flops 4040 | bytes 32320 | tf_op jit(solution)/shard_map/psum | solution.py:79
  177.9 1.1 fusion.134
  181.1 1.6 convolution_bitcast_fusion.1
  182.8 101.2 %all-reduce.1 = (f32[100,40]{0,1:T(8,128)S(1)}, f32[100,50]{0,1:T(8,128)S(1)}) all-reduce(f32[100,40]{0,1:T(8,128)S(1)} %fusion.60, f32[100,50]{0,1:T(8,128)S(1)} %fusion.64), channel_id=1, replica_groups=mesh['tx'=16,'ty'=32] {'tx','ty'}, use_global_device_ids=true, to_apply=%region_13.15 | all-reduce | flops 9000 | bytes 72000 | tf_op jit(solution)/shard_map/psum | solution.py:95
  284.0 359.7 %all-reduce.6.cloned.1.call-done = f32[100,40,50]{0,1,2:T(8,128)} async-done(((f32[100,40,50]{0,1,2:T(8,128)}), f32[100,40,50]{0,1,2:T(8,128)}) %all-reduce.6.cloned.1.call-update) | async-done | bytes 800016 | tf_op jit(solution)/shard_map/psum | solution.py:95
  643.8 1.4 multiply_reduce_fusion.1
  645.1 1.8 fusion.17
  648.8 103.1 %psum.68 = f32[100,40]{0,1:T(8,128)S(1)} all-reduce(f32[100,40]{0,1:T(8,128)S(1)} %fusion.31), channel_id=1, replica_groups=mesh['tx'=16,'ty'=32] {'tx','ty'}, use_global_device_ids=true, to_apply=%region_20.22 | all-reduce | flops 4000 | bytes 32000 | tf_op jit(solution)/shard_map/psum | solution.py:79
  751.9 1.1 fusion.136
  755.1 1.6 convolution_bitcast_fusion
  756.7 99.2 %all-reduce = (f32[100,40]{0,1:T(8,128)S(1)}, f32[100,50]{0,1:T(8,128)S(1)}) all-reduce(f32[100,40]{0,1:T(8,128)S(1)} %fusion.57, f32[100,50]{0,1:T(8,128)S(1)} %fusion.65), channel_id=1, replica_groups=mesh['tx'=16,'ty'=32] {'tx','ty'}, use_global_device_ids=true, to_apply=%region_24.26 | all-reduce | flops 9000 | bytes 72000 | tf_op jit(solution)/shard_map/psum | solution.py:95
  856.7 360.1 %all-reduce.8.cloned.1.call-done = f32[100,40,50]{0,1,2:T(8,128)} async-done(((f32[100,40,50]{0,1,2:T(8,128)}), f32[100,40,50]{0,1,2:T(8,128)}) %all-reduce.8.cloned.1.call-update) | async-done | bytes 800016 | tf_op jit(solution)/shard_map/psum | solution.py:95
  1216.8 1.4 multiply_reduce_fusion
  1218.2 1.8 fusion.13
  (122 shorter events, 20.2 us)
Async XLA Ops:
  7.2 636.6 %all-reduce.6.cloned.1.call-start = ((), (), s32[]{:S(2)}) async-start(), calls=%async_computation | async-start | bytes 2048000 | tf_op jit(solution)/shard_map/psum | solution.py:95
  7.2 14.1 %collective-permute-start = (f32[50,1,1,512]{3,2,1,0:T(1,128)}, f32[50,1,1,512]{3,2,1,0:T(1,128)S(1)}, u32[]{:S(2)}, u32[]{:S(2)}) collective-permute-start(f32[50,1,1,512]{3,2,1,0:T(1,128)} %param.7), channel_id=1, source_target_pairs={{0,32},{32,64},{64,96},{96,128},{128,160},{160,192},{192,224},{224... | collective-permute-start | bytes 307208 | tf_op jit(solution)/shard_map/ppermute | solution.py:20
  11.6 10.7 collective-permute-start.1
  22.3 8.5 collective-permute-start.3
  28.1 5.7 collective-permute-start.2
  55.6 6.6 copy-start
  58.5 5.4 copy-start.2
  59.3 5.6 copy-start.1
  62.2 117.3 %copy-start.3 = (f32[1,512]{1,0:T(1,128)S(1)}, f32[1,512]{1,0:T(1,128)}, u32[]{:S(2)}) copy-start(f32[1,512]{1,0:T(1,128)} %get-tuple-element.47) | copy-start | bytes 6148
  63.8 116.1 %copy-start.6 = (f32[1,512]{1,0:T(1,128)S(1)}, f32[1,512]{1,0:T(1,128)}, u32[]{:S(2)}) copy-start(f32[1,512]{1,0:T(1,128)} %get-tuple-element.48) | copy-start | bytes 6148
  64.9 115.4 %copy-start.5 = (f32[1,512]{1,0:T(1,128)S(1)}, f32[1,512]{1,0:T(1,128)}, u32[]{:S(2)}) copy-start(f32[1,512]{1,0:T(1,128)} %get-tuple-element.49) | copy-start | bytes 6148
  65.2 115.5 %copy-start.4 = (f32[1,512]{1,0:T(1,128)S(1)}, f32[1,512]{1,0:T(1,128)}, u32[]{:S(2)}) copy-start(f32[1,512]{1,0:T(1,128)} %get-tuple-element.46) | copy-start | bytes 6148
  182.7 1034.1 %all-reduce.8.cloned.1.call-start = ((), (), s32[]{:S(2)}) async-start(), calls=%async_computation.1 | async-start | bytes 2048000 | tf_op jit(solution)/shard_map/psum | solution.py:95
Sparse Core Ops, SparseCore 0:
  182.8 460.8 all-reduce.5
  756.9 459.9 all-reduce.7
where the time goes:
time: 1230 us
  waiting for transfers between devices  723 us (59%)
  blocking collectives  416 us (34%)
  local copies, waits for them, and re-layouts  30 us (2%)
  matrix products  17.1 us (1%)
  between operations  15.5 us (1%)
  other arithmetic  14.2 us (1%)
  starting transfers between devices  13.4 us (1%)
    psum x2, waiting for transfers between devices, per_device(): lax.psum((counts_part, sums_part, centre_part), ('tx', 'ty'))  720 us
    psum x2, blocking collectives, per_device(): occupied = lax.psum(jnp.dot(first, member.T, precision=HIGH), ('tx', 'ty'))  215 us
    psum x2, blocking collectives, per_device(): lax.psum((counts_part, sums_part, centre_part), ('tx', 'ty'))  200 us
  transfers between devices with their start and end apart: 6, of which 4 were waited for; matrix products, arithmetic and copies ran while one was open for 1% of the time, Pallas kernels for 0%

commit v1 on v0

v1 whole, which is shorter than its diff:
```python
import functools

import jax
import jax.numpy as jnp
from jax import lax
from jax.experimental import pallas as pl
from jax.experimental.pallas import tpu as pltpu
from jax.sharding import PartitionSpec as P

SLIDES = 40
SLOTS = 4
ITERS = 2
CLUSTERS = 100
PCS = 50
BOUND = 128
SHARPNESS = 20.0

LANES = 128
ROWS = 64
SENT = 56
ID_LANE = 126
LIVE_LANE = 127
NONE = -1000.0

F32 = jnp.float32
BF16 = jnp.bfloat16
HIGH = lax.Precision.HIGHEST
MESH = pl.DeviceIdType.MESH

NN = (((1,), (0,)), ((), ()))
NT = (((1,), (1,)), ((), ()))
TN = (((0,), (0,)), ((), ()))


def dot(a, b, dims):
    return lax.dot_general(a, b, dims, preferred_element_type=F32)


def dot_f32(a, b, dims):
    return lax.dot_general(a, b, dims, precision=HIGH, preferred_element_type=F32)


def split2(v):
    hi = v.astype(BF16)
    return hi, (v - hi.astype(F32)).astype(BF16)


def dot3(a, b, dims):
    ah, al = a if isinstance(a, tuple) else split2(a)
    bh, bl = split2(b)
    return dot(ah, bh, dims) + (dot(ah, bl, dims) + dot(al, bh, dims))


def iota(shape, dim):
    return lax.broadcasted_iota(jnp.int32, shape, dim)


class Sizes:
    def __init__(self, nx, ny):
        self.nx, self.ny = nx, ny
        self.gx = 8 if ny % 8 == 0 else 2
        self.gy = ny // self.gx
        self.dp = -(-PCS // ny)
        self.cr = self.dp * 8
        self.dense = (self.dp + 1) * SLIDES + self.dp
        self.dr = -(-self.dense // (nx * 8)) * 8
        self.drt = self.dr * nx


def kernel(
    sz, emb, nbr, sid, live, cent, out, outc,
    own, nb, cmat, zs, whi, wlo, cpad, e0, e2,
    f0, r0, f1, r1, f2, r2, s1, q1, s2, q2, s3, q3, s4, q4,
    halo_s, halo_r, ss, rs,
):
    nx, ny, gx, gy, dp, cr, dr = sz.nx, sz.ny, sz.gx, sz.gy, sz.dp, sz.cr, sz.dr
    cells = own.shape[1] - 8 * BOUND
    x, y = lax.axis_index("tx"), lax.axis_index("ty")

    def on_tx(r):
        return (lax.rem(x + r, nx), y)

    def on_ty(r):
        return (x, lax.rem(y + r, ny))

    def on_near(r):
        return (x, (y // gx) * gx + lax.rem(lax.rem(y, gx) + r, gx))

    def on_far(r):
        return (x, lax.rem(y + r * gx, ny))

    bar = pltpu.get_barrier_semaphore()

    def greet_ty(r, c):
        pl.semaphore_signal(bar, inc=1, device_id=on_ty(r), device_id_type=MESH)
        return c

    def greet_tx(r, c):
        pl.semaphore_signal(bar, inc=1, device_id=on_tx(r), device_id_type=MESH)
        return c

    lax.fori_loop(1, nx, greet_tx, 0)
    lax.fori_loop(1, ny, greet_ty, 0)
    for a in (1, nx - 1):
        for b in (1, ny - 1):
            pl.semaphore_signal(
                bar, inc=1, device_id=(lax.rem(x + a, nx), lax.rem(y + b, ny)), device_id_type=MESH
            )

    own[PCS:, :cells] = jnp.zeros((ROWS - PCS, cells), F32)
    own[:PCS, :cells] = emb[:, 0, 0, :]
    r0[:, :, SLOTS:, :] = jnp.zeros((ITERS, nx, 8 - SLOTS, LANES), F32)
    ids = nbr[:, 0, 0, :]
    center = 5 * BOUND + cells - BOUND
    ids = jnp.where(ids < center, ids, jnp.where(ids < center + BOUND, ids - center, ids - BOUND))
    for n in range(ids.shape[0]):
        nb[n] = jnp.broadcast_to(ids[n : n + 1, :], (8, cells))
    rows8 = iota((8, cells), 0)

    def count(g, c):
        base = rows8 + g * 16
        low = jnp.zeros((8, cells), F32)
        high = jnp.zeros((8, cells), F32)
        for n in range(ids.shape[0]):
            here = nb[n]
            low = low + jnp.where(here == base, 1.0, 0.0)
            high = high + jnp.where(here == base + 8, 1.0, 0.0)
        at = pl.multiple_of(g * 16, 16)
        cmat[pl.ds(at, 16), :] = jnp.concatenate([low, high], axis=0).astype(BF16)
        return c

    groups = cmat.shape[0] // 16
    lax.fori_loop(0, groups * 5 // 8, count, 0)

    pl.semaphore_wait(bar, nx - 1 + ny - 1 + 4)

    place = 0
    for a in (-1, 0, 1):
        for b in (-1, 0, 1):
            if a == 0 and b == 0:
                continue
            to = (lax.rem(x - a + nx, nx), lax.rem(y - b + ny, ny))
            pltpu.make_async_remote_copy(
                src_ref=own.at[pl.ds(0, SENT), pl.ds(0, BOUND)],
                dst_ref=own.at[pl.ds(0, SENT), pl.ds(cells + place * BOUND, BOUND)],
                send_sem=halo_s,
                recv_sem=halo_r,
                device_id=to,
                device_id_type=MESH,
            ).start()
            place += 1

    lax.fori_loop(groups * 5 // 8, groups, count, 0)

    alive = iota((1, cells), 1) < live[...]
    livef = alive.astype(F32)
    slides = sid[0].astype(F32)
    left = jnp.where(alive, slides, 64.0)
    masks, names = [], []
    for _ in range(SLOTS):
        name = jnp.min(left, axis=1, keepdims=True)
        masks.append(jnp.where(left == name, livef, 0.0))
        names.append(jnp.where(name < 64.0, name, NONE))
        left = jnp.where(left > name, left, 64.0)
    row = iota((8, cells), 0)
    zero = jnp.zeros((8, cells), F32)

    def stack(parts, first):
        total = zero
        for i, part in enumerate(parts):
            total = total + jnp.where(row == first + i, part, 0.0)
        return total

    mask8 = stack(masks, 0)
    masked = mask8 + stack([1.0 - livef], SLOTS)
    extra0 = stack(masks[:3], 5)
    extra1 = stack(masks[3:], 5)
    slot_row = iota((8, LANES), 0)
    slot_lane = iota((8, LANES), 1)
    name8 = jnp.full((8, LANES), NONE, F32)
    for i in range(SLOTS):
        name8 = jnp.where(slot_row == i, names[i], name8)
    here8 = (slot_lane.astype(F32) == name8).astype(F32)
    chunk_row = iota((cr, LANES), 0)
    chunk_lane = iota((cr, LANES), 1)
    chunk_name = jnp.zeros((cr, LANES), F32)
    for j in range(dp):
        for i in range(SLOTS):
            chunk_name = jnp.where(chunk_row == j * 8 + i, names[i], chunk_name)
    for i, at in enumerate((5, 6, 7, 13)):
        chunk_name = jnp.where(chunk_row == at, names[i], chunk_name)
    chunk_name = jnp.where(chunk_lane == ID_LANE, chunk_name, 0.0)

    cpad[...] = jnp.zeros_like(cpad)
    cpad[:CLUSTERS, :PCS] = cent[...]
    centre = cpad[...].T[:ROWS, :]

    pltpu.make_async_remote_copy(
        src_ref=own.at[pl.ds(0, SENT), pl.ds(cells, 8 * BOUND)],
        dst_ref=own.at[pl.ds(0, SENT), pl.ds(cells, 8 * BOUND)],
        send_sem=halo_s,
        recv_sem=halo_r,
        device_id=(x, lax.rem(y + 1, ny)),
        device_id_type=MESH,
    ).wait_recv()

    everything = own[...]
    part1 = everything.astype(BF16)
    rest = everything - part1.astype(F32)
    part2 = rest.astype(BF16)
    part3 = (rest - part2.astype(F32)).astype(BF16)
    summed = dot(jnp.concatenate([part1, part2, part3], axis=0), cmat[...], NN)
    summed = (summed[2 * ROWS :] + summed[ROWS : 2 * ROWS]) + summed[:ROWS]
    field = (everything[:, :cells] + summed) / (ids.shape[0] + 1.0)
    field = jnp.where(iota((ROWS, cells), 0) < PCS, field, 0.0) * livef

    cluster = iota((LANES, cells), 0)
    lane40 = iota((1, LANES), 1)

    def exchange(turn, phase, count_, begin, src, dst, to, region):
        sem = turn * 7 + phase

        def start(r, c):
            pltpu.make_async_remote_copy(
                src_ref=src(r), dst_ref=dst(r), send_sem=ss.at[sem], recv_sem=rs.at[sem],
                device_id=to(r), device_id_type=MESH,
            ).start()
            return c

        lax.fori_loop(1, count_, start, 0)
        return pltpu.make_async_remote_copy(
            src_ref=region, dst_ref=region, send_sem=ss.at[sem], recv_sem=rs.at[sem],
            device_id=to(1), device_id_type=MESH,
        )

    pending = []
    for turn in range(ITERS):
        unit_y = centre / jnp.sqrt(jnp.sum(centre * centre, axis=0, keepdims=True) + 1.0)
        inverse = 1.0 / jnp.sqrt(jnp.sum(field * field, axis=0, keepdims=True) + 1.0)
        unit_z = field * inverse
        zs[...] = field
        score = dot_f32(unit_y, unit_z, TN)
        raw = jnp.where(cluster < CLUSTERS, jnp.exp(SHARPNESS * (score - 1.0)), 0.0)
        first = raw * (livef / jnp.sum(raw, axis=0, keepdims=True))
        first = jnp.where(cluster == LIVE_LANE, livef, first)
        occ = dot_f32(mask8, first, NT)
        occ = jnp.where(slot_lane == ID_LANE, name8, occ)

        f0[turn] = occ
        r0[turn, 0, :SLOTS] = occ[:SLOTS]
        copy = exchange(
            turn, 0, nx, x,
            lambda r: f0.at[turn, pl.ds(0, SLOTS)],
            lambda r: r0.at[turn, r, pl.ds(0, SLOTS)],
            on_tx, r0.at[turn, pl.ds(1, nx - 1), pl.ds(0, SLOTS)],
        )

        m8 = mask8 + stack([inverse], SLOTS)

        def build(p, c):
            parts = []
            for j in range(dp):
                part = zs[pl.ds(p * dp + j, 1), :] * m8
                if j == 0:
                    part = part + extra0
                if j == 1:
                    part = part + extra1
                parts.append(part)
            both = jnp.concatenate(parts, axis=0)
            hi, lo = split2(both)
            at = pl.multiple_of(p * cr, cr)
            whi[pl.ds(at, cr), :] = hi
            wlo[pl.ds(at, cr), :] = lo
            return c

        lax.fori_loop(0, ny, build, 0)

        copy.wait_recv()
        pending.append(copy)
        got = r0[turn].reshape(nx * 8, LANES)
        if turn == 0:
            name = jnp.broadcast_to(got[:, ID_LANE : ID_LANE + 1], (nx * 8, LANES))
            lane = iota((nx * 8, LANES), 1).astype(F32)
            slot = lax.rem(iota((nx * 8, LANES), 0), 8)
            e0[...] = jnp.where((name == lane) & (slot < SLOTS), 1.0, 0.0).astype(BF16)
        hi, lo = split2(got)
        table = e0[...]
        part = (dot(table, lo, TN) + dot(table, hi, TN))[:SLIDES]
        f1[turn] = part
        r1[turn, 0] = part
        copy = exchange(
            turn, 1, gx, 0,
            lambda r: f1.at[turn],
            lambda r: r1.at[turn, r],
            on_near, r1.at[turn, pl.ds(1, gx - 1)],
        )
        copy.wait_recv()
        pending.append(copy)
        part = jnp.sum(r1[turn], axis=0)
        f2[turn] = part
        r2[turn, 0] = part
        copy = exchange(
            turn, 2, gy, 0,
            lambda r: f2.at[turn],
            lambda r: r2.at[turn, r],
            on_far, r2.at[turn, pl.ds(1, gy - 1)],
        )
        copy.wait_recv()
        pending.append(copy)
        occupied = jnp.sum(r2[turn], axis=0)
        totals = occupied[:, LIVE_LANE : LIVE_LANE + 1]
        expected = (
            jnp.sum(occupied, axis=0, keepdims=True)
            * totals
            / jnp.sum(totals, axis=0, keepdims=True)
        )
        ratio = (expected + 1.0) / (occupied + 1.0)
        ratio = jnp.where(lane40 < CLUSTERS, ratio * ratio, 1.0)
        mine = dot_f32(here8[:, :SLIDES], ratio, NN)
        mine = jnp.where(slot_row == SLOTS, 1.0, mine)
        weighted = raw * dot_f32(mine, masked, TN)
        assign = weighted * (livef / jnp.sum(weighted, axis=0, keepdims=True))

        ah, al = split2(assign)
        wide = dot(whi[...], jnp.concatenate([ah, al], axis=0), NT)
        sums = wide[:, :LANES] + (wide[:, LANES:] + dot(wlo[...], ah, NT))
        sums = sums.reshape(ny, cr, LANES) + chunk_name[None]
        s1[turn] = sums
        copy = exchange(
            turn, 3, ny, 0,
            lambda r: s1.at[turn, lax.rem(y + r, ny)],
            lambda r: q1.at[turn, r],
            on_ty, q1.at[turn, pl.ds(1, ny - 1)],
        )
        q1[turn, 0] = s1[turn, y]
        copy.wait_recv()
        pending.append(copy)
        got = q1[turn].reshape(ny * cr, LANES)
        if turn == 0:
            shape = (ny, cr, sz.drt)
            q = iota(shape, 1)
            j, c = q // 8, lax.rem(q, 8)
            named = (c < SLOTS) | ((j == 0) & (c > SLOTS)) | ((j == 1) & (c == 5))
            start = jnp.where(
                c < SLOTS,
                j * SLIDES,
                jnp.where(c == SLOTS, (dp + 1) * SLIDES + j, dp * SLIDES),
            ).astype(F32)
            name = got.reshape(ny, cr, LANES)[:, :, ID_LANE : ID_LANE + 1]
            goal = start + jnp.where(named, name, jnp.where(c == SLOTS, 0.0, NONE))
            table = jnp.where(goal == iota(shape, 2).astype(F32), 1.0, 0.0)
            e2[...] = table.reshape(ny * cr, sz.drt).astype(BF16)
        hi, lo = split2(got)
        table = e2[...]
        part = dot(table, lo, TN) + dot(table, hi, TN)
        s2[turn] = part.reshape(nx, dr, LANES)

        copy = exchange(
            turn, 4, nx, 0,
            lambda r: s2.at[turn, lax.rem(x + r, nx)],
            lambda r: q2.at[turn, r],
            on_tx, q2.at[turn, pl.ds(1, nx - 1)],
        )
        q2[turn, 0] = s2[turn, x]
        copy.wait_recv()
        pending.append(copy)
        part = jnp.sum(q2[turn], axis=0)
        s3[turn] = part
        q3[turn, x] = part
        copy = exchange(
            turn, 5, nx, 0,
            lambda r: s3.at[turn],
            lambda r: q3.at[turn, x],
            on_tx, q3.at[turn, pl.ds(1, nx - 1)],
        )
        copy.wait_recv()
        pending.append(copy)
        whole = q3[turn].reshape(sz.drt, LANES)
        counts = whole[dp * SLIDES : (dp + 1) * SLIDES]
        scale = 1.0 / (counts + 1.0)
        weight = jnp.sum(counts * scale, axis=0, keepdims=True)
        weight = jnp.where(lane40 < CLUSTERS, weight, 1.0)
        betas = []
        for j in range(dp):
            part = whole[j * SLIDES : (j + 1) * SLIDES]
            mean = jnp.sum(part * scale, axis=0, keepdims=True) / weight
            betas.append((part - counts * mean) * scale)
        betas.append(whole[dp * SLIDES :])
        hi, lo = split2(jnp.concatenate(betas, axis=0))
        chosen = dot(e2[...], jnp.concatenate([hi, lo], axis=1), NN)
        chosen = chosen[:, :LANES] + chosen[:, LANES:]
        s4[turn] = chosen.reshape(ny, cr, LANES)

        at = pl.multiple_of(y * cr, cr)
        copy = exchange(
            turn, 6, ny, 0,
            lambda r: s4.at[turn, r],
            lambda r: q4.at[turn, pl.ds(at, cr)],
            lambda r: on_ty(ny - r), q4.at[turn, pl.ds(cr, (ny - 1) * cr)],
        )
        q4[turn, pl.ds(at, cr)] = s4[turn, 0]
        copy.wait_recv()
        pending.append(copy)
        count_d = ny * dp
        slot_beta = [q4[turn, pl.ds(i, count_d, stride=8), :] for i in range(SLOTS)]
        shifts = dot3(jnp.concatenate(slot_beta, axis=0), assign, NN)
        shift = shifts[:count_d] * masks[0]
        for i in range(1, SLOTS):
            shift = shift + shifts[i * count_d : (i + 1) * count_d] * masks[i]
        centre = q4[turn, pl.ds(SLOTS, count_d, stride=8), :]
        if count_d < ROWS:
            shift = jnp.concatenate([shift, jnp.zeros((ROWS - count_d, cells), F32)], axis=0)
            centre = jnp.concatenate([centre, jnp.zeros((ROWS - count_d, LANES), F32)], axis=0)
        field = field - shift

    out[:, 0, 0, :] = field[:PCS]
    unit_y = centre / jnp.sqrt(jnp.sum(centre * centre, axis=0, keepdims=True) + 1.0)
    cpad[:ROWS, :] = unit_y
    outc[...] = cpad[...].T[:CLUSTERS, :PCS]

    pltpu.make_async_remote_copy(
        src_ref=own.at[pl.ds(0, SENT), pl.ds(cells, 8 * BOUND)],
        dst_ref=own.at[pl.ds(0, SENT), pl.ds(cells, 8 * BOUND)],
        send_sem=halo_s,
        recv_sem=halo_r,
        device_id=(x, lax.rem(y + 1, ny)),
        device_id_type=MESH,
    ).wait_send()
    for copy in pending:
        copy.wait_send()


def per_device(sz, embedding, neighbors, slide_id, live_count, centroids):
    cells = embedding.shape[3]
    near = neighbors.shape[0]
    nx, ny, cr, dr = sz.nx, sz.ny, sz.cr, sz.dr
    vmem = pl.BlockSpec(memory_space=pltpu.VMEM)

    def buf(*shape):
        return pltpu.VMEM((ITERS,) + shape, F32)

    return pl.pallas_call(
        functools.partial(kernel, sz),
        out_shape=(
            jax.ShapeDtypeStruct(embedding.shape, F32),
            jax.ShapeDtypeStruct(centroids.shape, F32),
        ),
        in_specs=[vmem] * 5,
        out_specs=(vmem, vmem),
        scratch_shapes=[
            pltpu.VMEM((ROWS, cells + 8 * BOUND), F32),
            pltpu.VMEM((near, 8, cells), jnp.int32),
            pltpu.VMEM((cells + 8 * BOUND, cells), BF16),
            pltpu.VMEM((ROWS, cells), F32),
            pltpu.VMEM((ny * cr, cells), BF16),
            pltpu.VMEM((ny * cr, cells), BF16),
            pltpu.VMEM((LANES, LANES), F32),
            pltpu.VMEM((nx * 8, LANES), BF16),
            pltpu.VMEM((ny * cr, sz.drt), BF16),
            buf(8, LANES),
            buf(nx, 8, LANES),
            buf(SLIDES, LANES),
            buf(sz.gx, SLIDES, LANES),
            buf(SLIDES, LANES),
            buf(sz.gy, SLIDES, LANES),
            buf(ny, cr, LANES),
            buf(ny, cr, LANES),
            buf(nx, dr, LANES),
            buf(nx, dr, LANES),
            buf(dr, LANES),
            buf(nx, dr, LANES),
            buf(ny, cr, LANES),
            buf(ny * cr, LANES),
            pltpu.SemaphoreType.DMA,
            pltpu.SemaphoreType.DMA,
            pltpu.SemaphoreType.DMA((7 * ITERS,)),
            pltpu.SemaphoreType.DMA((7 * ITERS,)),
        ],
        compiler_params=pltpu.CompilerParams(
            collective_id=0, has_side_effects=True, vmem_limit_bytes=48 * 1024 * 1024
        ),
        name="harmony",
    )(embedding, neighbors, slide_id, live_count, centroids)


def solution(mesh):
    sz = Sizes(mesh.shape["tx"], mesh.shape["ty"])
    placed = (
        P(None, "tx", "ty", None),
        P(None, "tx", "ty", None),
        P("tx", "ty", None),
        P("tx", "ty"),
        P(),
    )
    return jax.shard_map(
        functools.partial(per_device, sz),
        mesh=mesh,
        in_specs=placed,
        out_specs=(P(None, "tx", "ty", None), P()),
        check_vma=False,
    )
```

time: 1230 us -> 118 us (0.10)
  waiting for transfers between devices: 723 us -> 0 us
  blocking collectives: 416 us -> 0 us
  Pallas kernels: 0 us -> 114 us
  local copies, waits for them, and re-layouts: 30 us -> 3.1 us
  matrix products: 17.1 us -> 0 us
  other arithmetic: 14.2 us -> 0 us
  between operations: 15.5 us -> 1.32 us
  starting transfers between devices: 13.4 us -> 0 us
    psum x2 -> x0, waiting for transfers between devices: 720 us -> none  [per_device(): lax.psum((counts_part, sums_part, centre_part), ('tx', 'ty'))]
    psum x4 -> x0, blocking collectives: 416 us -> none  [the longest x2 215 us: per_device(): occupied = lax.psum(jnp.dot(first, member.T, precision=HIGH), ('tx', 'ty'))]
    pallas_call x0 -> x1, Pallas kernels: none -> 114 us  [per_device(): pl.pallas_call(functools.partial(kernel, sz), out_shape=(jax.ShapeDtypeSt...]
    gather x30 -> x0, local copies, waits for them, and re-layouts: 23.8 us -> none  [per_device(): total = total + jnp.take(source, position[step], axis=1)]
    dot_general x30 -> x0, matrix products: 17.1 us -> none  [the longest x2 3.51 us: per_device(): slot_beta = jnp.einsum('sb,kbd->skd', place, beta, precision=HIGH)]
    ppermute x4 -> x0, starting transfers between devices: 13.3 us -> none  [the longest x2 7 us: extended(): lax.ppermute(lax.slice_in_dim(block, 0, width, axis=dim), axis, backward)]
  transfers between devices with their start and end apart: 6 -> 0, of which waited for: 4 -> 0; matrix products, arithmetic and copies ran while one was open for 1% -> 0% of each run, Pallas kernels for 0% -> 0%
where the time goes in v1:
time: 118 us
  Pallas kernels  114 us (97%)
  local copies, waits for them, and re-layouts  3.1 us (3%)
  between operations  1.32 us (1%)
    pallas_call x1, Pallas kernels, per_device(): pl.pallas_call(functools.partial(kernel, sz), out_shape=(jax.ShapeDtypeSt...  114 us
    unnamed x8, local copies, waits for them, and re-layouts  2.4 us

profile of v1, /device:TPU:1, one launch (start us, length us, event | category | flops | bytes accessed | tf_op | source)
XLA Modules:
  0.0 118.2 jit_solution(2469358028339577856)
XLA Ops:
  1.3 0.0 copy-start.1
  1.3 0.0 copy-start.2
  1.3 0.9 copy.7.cent
  2.2 0.0 copy-done.1
  2.2 0.0 copy-done.2
  2.2 0.0 copy-start
  2.2 0.9 copy-done
  3.1 113.8 %harmony.1 = (f32[50,1,1,512]{3,2,1,0:T(1,128)S(1)}, f32[100,50]{1,0:T(8,128)S(1)}) custom-call(f32[50,1,1,512]{3,2,1,0:T(1,128)S(1)} %copy-done, s32[15,1,1,512]{3,2,1,0:T(1,128)S(1)} %copy-done.1, s32[1,1,512]{2,1,0:T(1,128)S(1)} %copy-done.2, s32[1,1]{1,0:T(1,128)S(6)} %copy.10.live, f32[100,50]{1,0:T(8,128)S(1)} %copy.7.cent), custom_call_target="tpu_custom_call" | custom-call | tf_op jit(solution)/shard_map/harmony/pallas_call | solution.py:442
  116.9 0.7 copy.8
  117.6 0.6 copy.11
Async XLA Ops:
  1.3 0.9 copy-start.1
  1.3 0.9 copy-start.2
  2.2 0.9 copy-start

commit v2 on v1

v2 whole, which is shorter than its diff:
```python
import functools

import jax
import jax.numpy as jnp
from jax import lax
from jax.experimental import pallas as pl
from jax.experimental.pallas import tpu as pltpu
from jax.sharding import PartitionSpec as P

SLIDES = 40
SLOTS = 4
ITERS = 2
CLUSTERS = 100
PCS = 50
BOUND = 128
SHARPNESS = 20.0

LANES = 128
ROWS = 56
PAIRS = 25
CHUNK = 16
SENT = 14
BACK = 10
ID_LANE = 126
LIVE_LANE = 127
NONE = -1000.0

F32 = jnp.float32
BF16 = jnp.bfloat16
HIGH = lax.Precision.HIGHEST
MESH = pl.DeviceIdType.MESH

NN = (((1,), (0,)), ((), ()))
NT = (((1,), (1,)), ((), ()))
TN = (((0,), (0,)), ((), ()))


def dot(a, b, dims):
    return lax.dot_general(a, b, dims, preferred_element_type=F32)


def dot_f32(a, b, dims):
    return lax.dot_general(a, b, dims, precision=HIGH, preferred_element_type=F32)


def split2(v):
    hi = v.astype(BF16)
    return hi, (v - hi.astype(F32)).astype(BF16)


def dot3(a, b, dims):
    ah, al = a if isinstance(a, tuple) else split2(a)
    bh, bl = split2(b)
    return dot(ah, bh, dims) + (dot(ah, bl, dims) + dot(al, bh, dims))


def iota(shape, dim):
    return lax.broadcasted_iota(jnp.int32, shape, dim)


SIDE = 4


def ring(a):
    return min(a, SIDE - a)


SQUARE = sorted(
    ((a, b) for a in range(SIDE) for b in range(SIDE)), key=lambda o: -ring(o[0]) - ring(o[1])
)
OTHERS = [(a, b, c) for a, b in SQUARE for c in (1, 0) if a or b or c]
NEAR = [(0, b, c) for b in (2, 1, 3, 0) for c in (1, 0) if b or c]
FAR = [(a, 0, 0) for a in (2, 1, 3)]
DENSE = 3 * SLIDES + 2


def slot_of(a, b, c):
    return (a * SIDE + b) * 2 + c


def kernel(
    nx, ny, emb, nbr, sid, live, cent, out, outc,
    embv, nbrv, own, nb, cmat, zs, whi, wlo, cpad, e0, e2,
    f0, r0, f1, r1, f2, r2, s1, q1, s2, q2, s3, q3, s4, q4,
    load, halo_s, halo_r, ss, rs, seen,
):
    cells = own.shape[1] - 8 * BOUND
    dr = s2.shape[2]
    x, y = lax.axis_index("tx"), lax.axis_index("ty")
    core, chip = lax.rem(y, 2), y // 2
    chip_y, chip_x = chip // SIDE, lax.rem(chip, SIDE)
    pair = core * (SIDE * SIDE) + chip
    across = sorted(range(1, nx), key=lambda r: -min(r, nx - r))

    def on_tx(r):
        return (lax.rem(x + r, nx), y)

    def on_ty(a, b, c):
        to = lax.rem(chip_y + a, SIDE) * SIDE + lax.rem(chip_x + b, SIDE)
        return (x, to * 2 + lax.rem(core + c, 2))

    get_ids = pltpu.make_async_copy(nbr, nbrv, load.at[0])
    get_ids.start()
    get_emb = pltpu.make_async_copy(emb, embv, load.at[1])
    get_emb.start()

    bar = pltpu.get_barrier_semaphore()

    def tile(a, b):
        return (lax.rem(x + a + nx, nx), lax.rem(y + b + ny, ny))

    def greet(sem, a, b):
        pl.semaphore_signal(sem, inc=1, device_id=tile(a, b), device_id_type=MESH)

    border = [(a, b) for a in (-1, 0, 1) for b in (-1, 0, 1) if a or b]
    first_met = border + [(a, 0) for a in (-3, -2, 2, 3)]
    for a, b in first_met:
        greet(bar, a, b)

    def greet_tx(step, d):
        for a in (-d, d):
            greet(seen.at[step], a, 0)

    def greet_ty(step, d):
        for b in (-d, d):
            greet(seen.at[step], 0, b)

    def heard(step):
        pl.semaphore_wait(seen.at[step], 2)

    r0[:, :, SLOTS:, :] = jnp.zeros((ITERS, nx, 8 - SLOTS, LANES), F32)
    q1[:, :, SENT:, :] = jnp.zeros((ITERS, ny, CHUNK - SENT, LANES), F32)
    q4[:, PAIRS * BACK :, :] = jnp.zeros((ITERS, q4.shape[1] - PAIRS * BACK, LANES), F32)
    cpad[...] = jnp.zeros_like(cpad)
    cpad[:PCS, :CLUSTERS] = cent[...]
    own[PCS:, :cells] = jnp.zeros((ROWS - PCS, cells), F32)
    get_ids.wait()
    ids = nbrv[:, 0, 0, :]
    center = 5 * BOUND + cells - BOUND
    ids = jnp.where(ids < center, ids, jnp.where(ids < center + BOUND, ids - center, ids - BOUND))
    for n in range(ids.shape[0]):
        nb[n] = jnp.broadcast_to(ids[n : n + 1, :], (8, cells))
    rows8 = iota((8, cells), 0)

    def count(g, c):
        base = rows8 + g * 16
        low = jnp.zeros((8, cells), F32)
        high = jnp.zeros((8, cells), F32)
        for n in range(ids.shape[0]):
            here = nb[n]
            low = low + jnp.where(here == base, 1.0, 0.0)
            high = high + jnp.where(here == base + 8, 1.0, 0.0)
        at = pl.multiple_of(g * 16, 16)
        cmat[pl.ds(at, 16), :] = jnp.concatenate([low, high], axis=0).astype(BF16)
        return c

    groups = cmat.shape[0] // 16
    early = groups * 7 // 16
    lax.fori_loop(0, early, count, 0)
    get_emb.wait()
    own[:PCS, :cells] = embv[:, 0, 0, :]

    pl.semaphore_wait(bar, len(first_met))

    for place, (a, b) in enumerate(border):
        pltpu.make_async_remote_copy(
            src_ref=own.at[:, pl.ds(0, BOUND)],
            dst_ref=own.at[:, pl.ds(cells + place * BOUND, BOUND)],
            send_sem=halo_s,
            recv_sem=halo_r,
            device_id=tile(-a, -b),
            device_id_type=MESH,
        ).start()
    halo = pltpu.make_async_remote_copy(
        src_ref=own.at[:, pl.ds(cells, 8 * BOUND)],
        dst_ref=own.at[:, pl.ds(cells, 8 * BOUND)],
        send_sem=halo_s,
        recv_sem=halo_r,
        device_id=on_tx(1),
        device_id_type=MESH,
    )

    greet_tx(0, 3)
    greet_ty(2, 1)
    lax.fori_loop(early, groups, count, 0)

    alive = iota((1, cells), 1) < live[...]
    livef = alive.astype(F32)
    slides = sid[0].astype(F32)
    left = jnp.where(alive, slides, 64.0)
    masks, names = [], []
    for _ in range(SLOTS):
        name = jnp.min(left, axis=1, keepdims=True)
        masks.append(jnp.where(left == name, livef, 0.0))
        names.append(jnp.where(name < 64.0, name, NONE))
        left = jnp.where(left > name, left, 64.0)
    row = iota((8, cells), 0)

    def stack(parts):
        total = jnp.zeros((8, cells), F32)
        for at, part in parts:
            total = total + jnp.where(row == at, part, 0.0)
        return total

    by_slot = list(enumerate(masks))
    mask8 = stack(by_slot)
    masked = stack(by_slot + [(SLOTS, 1.0 - livef)])
    slot_row = iota((8, LANES), 0)
    slot_lane = iota((8, LANES), 1)
    name8 = jnp.full((8, LANES), NONE, F32)
    for i in range(SLOTS):
        name8 = jnp.where(slot_row == i, names[i], name8)
    here8 = (slot_lane.astype(F32) == name8).astype(F32)
    chunk_row = iota((CHUNK, LANES), 0)
    chunk_lane = iota((CHUNK, LANES), 1)
    chunk_name = jnp.zeros((CHUNK, LANES), F32)
    for first in (0, 5, 10):
        for i in range(SLOTS):
            chunk_name = jnp.where(chunk_row == first + i, names[i], chunk_name)
    chunk_name = jnp.where(chunk_lane == ID_LANE, chunk_name, 0.0)
    centre = cpad[...]

    heard(0)
    greet_tx(1, 2)
    heard(2)
    greet_ty(3, 2)
    halo.wait_recv()
    everything = own[...]
    part1 = everything.astype(BF16).astype(F32)
    rest = everything - part1
    part2 = rest.astype(BF16).astype(F32)
    parts = jnp.concatenate([part1, part2, rest - part2], axis=0).astype(BF16)
    summed = dot(parts, cmat[...], NN)
    summed = (summed[2 * ROWS :] + summed[ROWS : 2 * ROWS]) + summed[:ROWS]
    field = (everything[:, :cells] + summed) / (ids.shape[0] + 1.0)
    field = jnp.where(iota((ROWS, cells), 0) < PCS, field, 0.0) * livef

    heard(3)
    greet_ty(4, 4)
    heard(1)

    cluster = iota((LANES, cells), 0)
    lane40 = iota((1, LANES), 1)

    def sender(sem):
        def send(src, dst, to):
            pltpu.make_async_remote_copy(
                src_ref=src, dst_ref=dst, send_sem=ss.at[sem], recv_sem=rs.at[sem],
                device_id=to, device_id_type=MESH,
            ).start()

        return send

    def arrivals(sem, region):
        return pltpu.make_async_remote_copy(
            src_ref=region, dst_ref=region, send_sem=ss.at[sem], recv_sem=rs.at[sem],
            device_id=on_tx(1), device_id_type=MESH,
        )

    pending = []
    at_pairs = []
    for turn in range(ITERS):
        sem = turn * 7
        unit_y = centre / jnp.sqrt(jnp.sum(centre * centre, axis=0, keepdims=True) + 1.0)
        inverse = 1.0 / jnp.sqrt(jnp.sum(field * field, axis=0, keepdims=True) + 1.0)
        unit_z = field * inverse
        zs[...] = field
        score = dot_f32(unit_y, unit_z, TN)
        raw = jnp.where(cluster < CLUSTERS, jnp.exp(SHARPNESS * (score - 1.0)), 0.0)
        first = raw * (livef / jnp.sum(raw, axis=0, keepdims=True))
        first = jnp.where(cluster == LIVE_LANE, livef, first)
        occ = dot_f32(mask8, first, NT)
        occ = jnp.where(slot_lane == ID_LANE, name8, occ)

        f0[turn] = occ
        send = sender(sem)
        for r in across:
            send(f0.at[turn, pl.ds(0, SLOTS)], r0.at[turn, r, pl.ds(0, SLOTS)], on_tx(r))
        r0[turn, 0, :SLOTS] = occ[:SLOTS]

        if turn == 0:
            heard(4)
            greet_ty(5, 8)

        slots_a = stack(by_slot + [(4, inverse)] + [(5 + i, masks[i]) for i in range(3)])
        slots_b = stack([(0, masks[3]), (1, inverse)])
        ones_b = stack([(2 + i, masks[i]) for i in range(SLOTS)])

        def build(p, c):
            one = zs[pl.ds(p * 2, 1), :]
            two = zs[pl.ds(p * 2 + 1, 1), :]
            upper = jnp.where(row < 5, one, two) * slots_a
            lower = two * slots_b + ones_b
            hi, lo = split2(jnp.concatenate([upper, lower], axis=0))
            at = pl.multiple_of(p * CHUNK, CHUNK)
            whi[pl.ds(at, CHUNK), :] = hi
            wlo[pl.ds(at, CHUNK), :] = lo
            return c

        lax.fori_loop(0, PAIRS, build, 0)

        if turn == 0:
            heard(5)
        copy = arrivals(sem, r0.at[turn, pl.ds(1, nx - 1), pl.ds(0, SLOTS)])
        copy.wait_recv()
        pending.append(copy)
        got = r0[turn].reshape(nx * 8, LANES)
        if turn == 0:
            name = jnp.broadcast_to(got[:, ID_LANE : ID_LANE + 1], (nx * 8, LANES))
            lane = iota((nx * 8, LANES), 1).astype(F32)
            slot = lax.rem(iota((nx * 8, LANES), 0), 8)
            e0[...] = jnp.where((name == lane) & (slot < SLOTS), 1.0, 0.0).astype(BF16)
        hi, lo = split2(got)
        table = e0[...]
        part = (dot(table, lo, TN) + dot(table, hi, TN))[:SLIDES]
        f1[turn] = part
        send = sender(sem + 1)
        for offset in NEAR:
            send(f1.at[turn], r1.at[turn, slot_of(*offset)], on_ty(*offset))
        r1[turn, 0] = part
        copy = arrivals(sem + 1, r1.at[turn, pl.ds(1, len(NEAR))])
        copy.wait_recv()
        pending.append(copy)
        part = jnp.sum(r1[turn], axis=0)
        f2[turn] = part
        send = sender(sem + 2)
        for offset in FAR:
            send(f2.at[turn], r2.at[turn, offset[0]], on_ty(*offset))
        r2[turn, 0] = part
        copy = arrivals(sem + 2, r2.at[turn, pl.ds(1, len(FAR))])
        copy.wait_recv()
        pending.append(copy)
        occupied = jnp.sum(r2[turn], axis=0)
        totals = occupied[:, LIVE_LANE : LIVE_LANE + 1]
        expected = (
            jnp.sum(occupied, axis=0, keepdims=True)
            * totals
            / jnp.sum(totals, axis=0, keepdims=True)
        )
        ratio = (expected + 1.0) / (occupied + 1.0)
        ratio = jnp.where(lane40 < CLUSTERS, ratio * ratio, 1.0)
        mine = dot_f32(here8[:, :SLIDES], ratio, NN)
        mine = jnp.where(slot_row == SLOTS, 1.0, mine)
        weighted = raw * dot_f32(mine, masked, TN)
        assign = weighted * (livef / jnp.sum(weighted, axis=0, keepdims=True))

        ah, al = split2(assign)
        both = jnp.concatenate([ah, al], axis=0)
        send = sender(sem + 3)
        chips = SIDE * SIDE
        for side, count_ in ((0, chips), (1, PAIRS - chips)):
            rows = pl.ds(side * chips * CHUNK, count_ * CHUNK)
            wide = dot(whi[rows, :], both, NT)
            sums = wide[:, :LANES] + (wide[:, LANES:] + dot(wlo[rows, :], ah, NT))
            sums = sums.reshape(count_, CHUNK, LANES) + chunk_name[None]
            s1[turn, pl.ds(side * chips, count_)] = sums
            c = lax.rem(core + side, 2)
            for a, b in SQUARE:
                to = lax.rem(chip_y + a, SIDE) * SIDE + lax.rem(chip_x + b, SIDE)

                def go(a=a, b=b, to=to, c=c, side=side):
                    send(
                        s1.at[turn, side * chips + to, pl.ds(0, SENT)],
                        q1.at[turn, (a * SIDE + b) * 2 + c, pl.ds(0, SENT)],
                        (x, to * 2 + side),
                    )

                if side == 0 and (a or b):
                    go()
                elif side == 0:
                    pl.when(core != side)(go)
                elif a or b:
                    pl.when(to < count_)(go)
                else:
                    pl.when((core != side) & (to < count_))(go)

        @pl.when(pair < PAIRS)
        def _():
            q1[turn, 0, :SENT] = s1[turn, pair, :SENT]
            arrivals(sem + 3, q1.at[turn, pl.ds(1, ny - 1), pl.ds(0, SENT)]).wait_recv()
            got = q1[turn].reshape(ny * CHUNK, LANES)
            if turn == 0:
                shape = (ny * CHUNK, LANES)
                at = lax.rem(iota(shape, 0), CHUNK)
                second = (at >= 5) & (at < 10)
                middle = (at == 4) | (at == 9)
                start = jnp.where(
                    middle,
                    3 * SLIDES + second.astype(jnp.int32),
                    jnp.where(second, SLIDES, jnp.where(at >= 10, 2 * SLIDES, 0)),
                ).astype(F32)
                name = jnp.broadcast_to(got[:, ID_LANE : ID_LANE + 1], shape)
                name = jnp.where(middle, 0.0, jnp.where(at < SENT, name, NONE))
                goal = start + name
                table = jnp.where(goal == iota(shape, 1).astype(F32), 1.0, 0.0)
                e2[...] = table.astype(BF16)
            hi, lo = split2(got)
            table = e2[...]
            part = dot(table, lo, TN) + dot(table, hi, TN)
            s2[turn] = part.reshape(nx, dr, LANES)

            send = sender(sem + 4)
            for r in across:
                send(s2.at[turn, lax.rem(x + r, nx)], q2.at[turn, r], on_tx(r))
            q2[turn, 0] = s2[turn, x]
            arrivals(sem + 4, q2.at[turn, pl.ds(1, nx - 1)]).wait_recv()
            part = jnp.sum(q2[turn], axis=0)
            s3[turn] = part
            send = sender(sem + 5)
            for r in across:
                send(s3.at[turn], q3.at[turn, x], on_tx(r))
            q3[turn, x] = part
            arrivals(sem + 5, q3.at[turn, pl.ds(1, nx - 1)]).wait_recv()
            whole = q3[turn].reshape(nx * dr, LANES)
            counts = whole[2 * SLIDES : 3 * SLIDES]
            scale = 1.0 / (counts + 1.0)
            weight = jnp.sum(counts * scale, axis=0, keepdims=True)
            weight = jnp.where(lane40 < CLUSTERS, weight, 1.0)
            betas = []
            for j in range(2):
                part = whole[j * SLIDES : (j + 1) * SLIDES]
                mean = jnp.sum(part * scale, axis=0, keepdims=True) / weight
                betas.append((part - counts * mean) * scale)
            betas.append(whole[2 * SLIDES :])
            hi, lo = split2(jnp.concatenate(betas, axis=0))
            chosen = dot(e2[...], jnp.concatenate([hi, lo], axis=1), NN)
            chosen = chosen[:, :LANES] + chosen[:, LANES:]
            s4[turn] = chosen.reshape(ny, CHUNK, LANES)

            send = sender(sem + 6)
            for a, b, c in OTHERS:
                send(
                    s4.at[turn, slot_of(a, b, c), pl.ds(0, BACK)],
                    q4.at[turn, pl.ds(pair * BACK, BACK)],
                    on_ty(SIDE - a, SIDE - b, 2 - c),
                )
            q4[turn, pl.ds(pair * BACK, BACK)] = s4[turn, 0, :BACK]
            arrivals(sem + 6, q4.at[turn, pl.ds(0, (PAIRS - 1) * BACK)]).wait_recv()

        @pl.when(pair >= PAIRS)
        def _():
            arrivals(sem + 6, q4.at[turn, pl.ds(0, PAIRS * BACK)]).wait_recv()

        slot_beta = [q4[turn, pl.ds(i, ROWS, stride=5), :] for i in range(SLOTS)]
        shifts = dot3(jnp.concatenate(slot_beta, axis=0), assign, NN)
        for i in range(SLOTS):
            field = field - shifts[i * ROWS : (i + 1) * ROWS] * masks[i]
        centre = q4[turn, pl.ds(SLOTS, ROWS, stride=5), :]

    out[:, 0, 0, :] = field[:PCS]
    unit_y = centre / jnp.sqrt(jnp.sum(centre * centre, axis=0, keepdims=True) + 1.0)
    outc[...] = unit_y[:PCS, :CLUSTERS]

    halo.wait_send()
    for copy in pending:
        copy.wait_send()
    for turn in range(ITERS):
        sem = turn * 7

        @pl.when(pair < PAIRS)
        def _():
            arrivals(sem + 3, q1.at[turn, pl.ds(0, PAIRS - 1), pl.ds(0, SENT)]).wait_send()
            arrivals(sem + 4, q2.at[turn, pl.ds(1, nx - 1)]).wait_send()
            arrivals(sem + 5, q3.at[turn, pl.ds(1, nx - 1)]).wait_send()
            arrivals(sem + 6, s4.at[turn, pl.ds(1, ny - 1), pl.ds(0, BACK)]).wait_send()

        @pl.when(pair >= PAIRS)
        def _():
            arrivals(sem + 3, q1.at[turn, pl.ds(0, PAIRS), pl.ds(0, SENT)]).wait_send()


def per_device(nx, ny, embedding, neighbors, slide_id, live_count, centroids):
    cells = embedding.shape[3]
    near = neighbors.shape[0]
    dr = -(-DENSE // (nx * 8)) * 8
    vmem = pl.BlockSpec(memory_space=pltpu.VMEM)
    hbm = pl.BlockSpec(memory_space=pltpu.HBM)

    def buf(*shape):
        return pltpu.VMEM((ITERS,) + shape, F32)

    corrected, centers = pl.pallas_call(
        functools.partial(kernel, nx, ny),
        out_shape=(
            jax.ShapeDtypeStruct(embedding.shape, F32),
            jax.ShapeDtypeStruct((PCS, CLUSTERS), F32),
        ),
        in_specs=[hbm, hbm, vmem, vmem, vmem],
        out_specs=(vmem, vmem),
        scratch_shapes=[
            pltpu.VMEM(embedding.shape, F32),
            pltpu.VMEM(neighbors.shape, jnp.int32),
            pltpu.VMEM((ROWS, cells + 8 * BOUND), F32),
            pltpu.VMEM((near, 8, cells), jnp.int32),
            pltpu.VMEM((cells + 8 * BOUND, cells), BF16),
            pltpu.VMEM((ROWS, cells), F32),
            pltpu.VMEM((PAIRS * CHUNK, cells), BF16),
            pltpu.VMEM((PAIRS * CHUNK, cells), BF16),
            pltpu.VMEM((ROWS, LANES), F32),
            pltpu.VMEM((nx * 8, LANES), BF16),
            pltpu.VMEM((ny * CHUNK, LANES), BF16),
            buf(8, LANES),
            buf(nx, 8, LANES),
            buf(SLIDES, LANES),
            buf(len(NEAR) + 1, SLIDES, LANES),
            buf(SLIDES, LANES),
            buf(len(FAR) + 1, SLIDES, LANES),
            buf(PAIRS, CHUNK, LANES),
            buf(ny, CHUNK, LANES),
            buf(nx, dr, LANES),
            buf(nx, dr, LANES),
            buf(dr, LANES),
            buf(nx, dr, LANES),
            buf(ny, CHUNK, LANES),
            buf(ROWS * 5 + 8, LANES),
            pltpu.SemaphoreType.DMA((2,)),
            pltpu.SemaphoreType.DMA,
            pltpu.SemaphoreType.DMA,
            pltpu.SemaphoreType.DMA((7 * ITERS,)),
            pltpu.SemaphoreType.DMA((7 * ITERS,)),
            pltpu.SemaphoreType.REGULAR((6,)),
        ],
        compiler_params=pltpu.CompilerParams(
            collective_id=0, has_side_effects=True, vmem_limit_bytes=48 * 1024 * 1024
        ),
        name="harmony",
    )(embedding, neighbors, slide_id, live_count, centroids.T)
    return corrected, centers.T


def solution(mesh):
    nx, ny = mesh.shape["tx"], mesh.shape["ty"]
    placed = (
        P(None, "tx", "ty", None),
        P(None, "tx", "ty", None),
        P("tx", "ty", None),
        P("tx", "ty"),
        P(),
    )
    return jax.shard_map(
        functools.partial(per_device, nx, ny),
        mesh=mesh,
        in_specs=placed,
        out_specs=(P(None, "tx", "ty", None), P()),
        check_vma=False,
    )
```

time: 118 us -> 109 us (0.924)
  Pallas kernels: 114 us -> 104 us
    pallas_call x1, Pallas kernels: 114 us -> 104 us  [per_device(): pl.pallas_call(functools.partial(kernel, nx, ny), out_shape=(jax.ShapeDty...]
    unnamed x8 -> x10, local copies, waits for them, and re-layouts: 2.4 us -> 3.66 us
where the time goes in v2:
time: 109 us
  Pallas kernels  104 us (95%)
  local copies, waits for them, and re-layouts  3.66 us (3%)
  between operations  1.31 us (1%)
    pallas_call x1, Pallas kernels, per_device(): pl.pallas_call(functools.partial(kernel, nx, ny), out_shape=(jax.ShapeDty...  104 us
    unnamed x10, local copies, waits for them, and re-layouts  3.66 us

profile of v2, /device:TPU:1, one launch (start us, length us, event | category | flops | bytes accessed | tf_op | source)
XLA Modules:
  0.0 109.1 jit_solution(2255945084614929766)
XLA Ops:
  0.6 0.0 copy-start.3
  1.3 0.0 copy-done.3
  1.3 0.0 copy-start
  1.3 0.9 copy-done
  2.2 0.0 copy-start.1
  2.2 0.8 copy-done.1
  3.0 0.0 copy-start.2
  3.0 0.7 copy-done.2
  3.7 104.1 %harmony.1 = (f32[50,1,1,512]{3,2,1,0:T(1,128)S(1)}, f32[50,100]{1,0:T(8,128)S(1)}) custom-call(f32[50,1,1,512]{3,2,1,0:T(1,128)S(1)} %copy-done, s32[15,1,1,512]{3,2,1,0:T(1,128)S(1)} %copy-done.1, s32[1,1,512]{2,1,0:T(1,128)S(1)} %copy-done.3, s32[1,1]{1,0:T(1,128)S(6)} %copy.9.live, f32[50,100]{1,0:T(8,128)S(1)} %bitcast.2), custom_call_target="tpu_custom_call" | custom-call | tf_op jit(solution)/shard_map/harmony/pallas_call | solution.py:482
  107.8 0.6 copy.10
  108.5 0.6 copy.11
Async XLA Ops:
  0.6 0.7 copy-start.3
  1.3 0.9 copy-start
  2.2 0.8 copy-start.1
  3.0 0.7 copy-start.2

commit v3 on v2

--- a/solution.py
+++ b/solution.py
@@ -21,13 +21,14 @@
 CHUNK = 16
 SENT = 14
 BACK = 10
+HALF = 20
+PADDED = 24
 ID_LANE = 126
 LIVE_LANE = 127
 NONE = -1000.0
 
 F32 = jnp.float32
 BF16 = jnp.bfloat16
-HIGH = lax.Precision.HIGHEST
 MESH = pl.DeviceIdType.MESH
 
 NN = (((1,), (0,)), ((), ()))
@@ -39,19 +40,22 @@
     return lax.dot_general(a, b, dims, preferred_element_type=F32)
 
 
-def dot_f32(a, b, dims):
-    return lax.dot_general(a, b, dims, precision=HIGH, preferred_element_type=F32)
-
-
 def split2(v):
     hi = v.astype(BF16)
     return hi, (v - hi.astype(F32)).astype(BF16)
 
 
-def dot3(a, b, dims):
-    ah, al = a if isinstance(a, tuple) else split2(a)
-    bh, bl = split2(b)
-    return dot(ah, bh, dims) + (dot(ah, bl, dims) + dot(al, bh, dims))
+def halves(v):
+    return v[:, :LANES] + v[:, LANES:]
+
+
+def split_lanes(v):
+    return jnp.concatenate(split2(v), axis=1)
+
+
+def parts_of(v):
+    hi = v.astype(BF16).astype(F32)
+    return hi, v - hi
 
 
 def iota(shape, dim):
@@ -74,14 +78,23 @@
 DENSE = 3 * SLIDES + 2
 
 
+def dense_row(name):
+    return jnp.where(name >= HALF, name + (PADDED - HALF), name)
+
+
+def place_of(a, b):
+    at = (a + 1) * 3 + b + 1
+    return at - (at > 4)
+
+
 def slot_of(a, b, c):
     return (a * SIDE + b) * 2 + c
 
 
 def kernel(
     nx, ny, emb, nbr, sid, live, cent, out, outc,
-    embv, nbrv, own, nb, cmat, zs, whi, wlo, cpad, e0, e2,
-    f0, r0, f1, r1, f2, r2, s1, q1, s2, q2, s3, q3, s4, q4,
+    embv, nbrv, sidv, centv, own, nb, cmat, zs, whi, wlo, cpad, e0, e2,
+    f0, r0, f1, r1, f2, r2, f3, r3, s1, q1, s2, q2, s3, q3, s4, q4,
     load, halo_s, halo_r, ss, rs, seen,
 ):
     cells = own.shape[1] - 8 * BOUND
@@ -103,6 +116,10 @@
     get_ids.start()
     get_emb = pltpu.make_async_copy(emb, embv, load.at[1])
     get_emb.start()
+    get_sid = pltpu.make_async_copy(sid, sidv, load.at[2])
+    get_sid.start()
+    get_cent = pltpu.make_async_copy(cent, centv, load.at[3])
+    get_cent.start()
 
     bar = pltpu.get_barrier_semaphore()
 
@@ -112,7 +129,7 @@
     def greet(sem, a, b):
         pl.semaphore_signal(sem, inc=1, device_id=tile(a, b), device_id_type=MESH)
 
-    border = [(a, b) for a in (-1, 0, 1) for b in (-1, 0, 1) if a or b]
+    border = [(a, b) for a in (-1, 1) for b in (-1, 1)] + [(-1, 0), (1, 0), (0, -1), (0, 1)]
     first_met = border + [(a, 0) for a in (-3, -2, 2, 3)]
     for a, b in first_met:
         greet(bar, a, b)
@@ -129,10 +146,12 @@
         pl.semaphore_wait(seen.at[step], 2)
 
     r0[:, :, SLOTS:, :] = jnp.zeros((ITERS, nx, 8 - SLOTS, LANES), F32)
+    r1[:, HALF:, :] = jnp.zeros((ITERS, PADDED - HALF, LANES), F32)
+    r2[:, :, HALF:, :] = jnp.zeros((ITERS, SIDE * SIDE, PADDED - HALF, LANES), F32)
+    r3[:, :, HALF:, :] = jnp.zeros((ITERS, 2, PADDED - HALF, LANES), F32)
     q1[:, :, SENT:, :] = jnp.zeros((ITERS, ny, CHUNK - SENT, LANES), F32)
     q4[:, PAIRS * BACK :, :] = jnp.zeros((ITERS, q4.shape[1] - PAIRS * BACK, LANES), F32)
     cpad[...] = jnp.zeros_like(cpad)
-    cpad[:PCS, :CLUSTERS] = cent[...]
     own[PCS:, :cells] = jnp.zeros((ROWS - PCS, cells), F32)
     get_ids.wait()
     ids = nbrv[:, 0, 0, :]
@@ -155,17 +174,17 @@
         return c
 
     groups = cmat.shape[0] // 16
-    early = groups * 7 // 16
+    early = groups * 10 // 16
     lax.fori_loop(0, early, count, 0)
     get_emb.wait()
     own[:PCS, :cells] = embv[:, 0, 0, :]
 
     pl.semaphore_wait(bar, len(first_met))
 
-    for place, (a, b) in enumerate(border):
+    for a, b in border:
         pltpu.make_async_remote_copy(
             src_ref=own.at[:, pl.ds(0, BOUND)],
-            dst_ref=own.at[:, pl.ds(cells + place * BOUND, BOUND)],
+            dst_ref=own.at[:, pl.ds(cells + place_of(a, b) * BOUND, BOUND)],
             send_sem=halo_s,
             recv_sem=halo_r,
             device_id=tile(-a, -b),
@@ -186,7 +205,8 @@
 
     alive = iota((1, cells), 1) < live[...]
     livef = alive.astype(F32)
-    slides = sid[0].astype(F32)
+    get_sid.wait()
+    slides = sidv[0].astype(F32)
     left = jnp.where(alive, slides, 64.0)
     masks, names = [], []
     for _ in range(SLOTS):
@@ -204,13 +224,15 @@
 
     by_slot = list(enumerate(masks))
     mask8 = stack(by_slot)
+    mask8_bf = mask8.astype(BF16)
     masked = stack(by_slot + [(SLOTS, 1.0 - livef)])
+    masked2 = jnp.concatenate([masked, masked], axis=0).astype(BF16)
     slot_row = iota((8, LANES), 0)
     slot_lane = iota((8, LANES), 1)
     name8 = jnp.full((8, LANES), NONE, F32)
     for i in range(SLOTS):
-        name8 = jnp.where(slot_row == i, names[i], name8)
-    here8 = (slot_lane.astype(F32) == name8).astype(F32)
+        name8 = jnp.where(slot_row == i, dense_row(names[i]), name8)
+    here8_bf = jnp.where(slot_lane.astype(F32) == name8, 1.0, 0.0)[:, : 2 * PADDED].astype(BF16)
     chunk_row = iota((CHUNK, LANES), 0)
     chunk_lane = iota((CHUNK, LANES), 1)
     chunk_name = jnp.zeros((CHUNK, LANES), F32)
@@ -218,6 +240,8 @@
         for i in range(SLOTS):
             chunk_name = jnp.where(chunk_row == first + i, names[i], chunk_name)
     chunk_name = jnp.where(chunk_lane == ID_LANE, chunk_name, 0.0)
+    get_cent.wait()
+    cpad[:PCS, :CLUSTERS] = centv[...]
     centre = cpad[...]
 
     heard(0)
@@ -260,16 +284,22 @@
     pending = []
     at_pairs = []
     for turn in range(ITERS):
-        sem = turn * 7
-        unit_y = centre / jnp.sqrt(jnp.sum(centre * centre, axis=0, keepdims=True) + 1.0)
-        inverse = 1.0 / jnp.sqrt(jnp.sum(field * field, axis=0, keepdims=True) + 1.0)
+        sem = turn * 8
+        unit_y = centre * lax.rsqrt(jnp.sum(centre * centre, axis=0, keepdims=True) + 1.0)
+        inverse = lax.rsqrt(jnp.sum(field * field, axis=0, keepdims=True) + 1.0)
         unit_z = field * inverse
         zs[...] = field
-        score = dot_f32(unit_y, unit_z, TN)
+        yh, yl = parts_of(unit_y)
+        zh, zl = parts_of(unit_z)
+        score = dot(
+            jnp.concatenate([yh, yh, yl, yl], axis=0).astype(BF16),
+            jnp.concatenate([zh, zl, zh, zl], axis=0).astype(BF16),
+            TN,
+        )
         raw = jnp.where(cluster < CLUSTERS, jnp.exp(SHARPNESS * (score - 1.0)), 0.0)
         first = raw * (livef / jnp.sum(raw, axis=0, keepdims=True))
         first = jnp.where(cluster == LIVE_LANE, livef, first)
-        occ = dot_f32(mask8, first, NT)
+        occ = halves(dot(mask8_bf, jnp.concatenate(split2(first), axis=0), NT))
         occ = jnp.where(slot_lane == ID_LANE, name8, occ)
 
         f0[turn] = occ
@@ -310,27 +340,35 @@
             lane = iota((nx * 8, LANES), 1).astype(F32)
             slot = lax.rem(iota((nx * 8, LANES), 0), 8)
             e0[...] = jnp.where((name == lane) & (slot < SLOTS), 1.0, 0.0).astype(BF16)
-        hi, lo = split2(got)
-        table = e0[...]
-        part = (dot(table, lo, TN) + dot(table, hi, TN))[:SLIDES]
-        f1[turn] = part
+        part = halves(dot(e0[...], split_lanes(got), TN)[: 2 * PADDED])
+        f1[turn] = part.reshape(2, PADDED, LANES)
         send = sender(sem + 1)
-        for offset in NEAR:
-            send(f1.at[turn], r1.at[turn, slot_of(*offset)], on_ty(*offset))
-        r1[turn, 0] = part
-        copy = arrivals(sem + 1, r1.at[turn, pl.ds(1, len(NEAR))])
+        send(f1.at[turn, 1 - core, pl.ds(0, HALF)], r1.at[turn, pl.ds(0, HALF)], on_ty(0, 0, 1))
+        copy = arrivals(sem + 1, r1.at[turn, pl.ds(0, HALF)])
         copy.wait_recv()
         pending.append(copy)
-        part = jnp.sum(r1[turn], axis=0)
+        part = r1[turn] + f1[turn, core]
         f2[turn] = part
         send = sender(sem + 2)
-        for offset in FAR:
-            send(f2.at[turn], r2.at[turn, offset[0]], on_ty(*offset))
+        for a, b in SQUARE[:-1]:
+            send(
+                f2.at[turn, pl.ds(0, HALF)],
+                r2.at[turn, a * SIDE + b, pl.ds(0, HALF)],
+                on_ty(a, b, 0),
+            )
         r2[turn, 0] = part
-        copy = arrivals(sem + 2, r2.at[turn, pl.ds(1, len(FAR))])
+        copy = arrivals(sem + 2, r2.at[turn, pl.ds(1, SIDE * SIDE - 1), pl.ds(0, HALF)])
         copy.wait_recv()
         pending.append(copy)
-        occupied = jnp.sum(r2[turn], axis=0)
+        part = jnp.sum(r2[turn], axis=0)
+        f3[turn] = part
+        send = sender(sem + 7)
+        send(f3.at[turn, pl.ds(0, HALF)], r3.at[turn, core, pl.ds(0, HALF)], on_ty(0, 0, 1))
+        r3[turn, core] = part
+        copy = arrivals(sem + 7, r3.at[turn, 0, pl.ds(0, HALF)])
+        copy.wait_recv()
+        pending.append(copy)
+        occupied = r3[turn].reshape(2 * PADDED, LANES)
         totals = occupied[:, LIVE_LANE : LIVE_LANE + 1]
         expected = (
             jnp.sum(occupied, axis=0, keepdims=True)
@@ -339,9 +377,10 @@
         )
         ratio = (expected + 1.0) / (occupied + 1.0)
         ratio = jnp.where(lane40 < CLUSTERS, ratio * ratio, 1.0)
-        mine = dot_f32(here8[:, :SLIDES], ratio, NN)
-        mine = jnp.where(slot_row == SLOTS, 1.0, mine)
-        weighted = raw * dot_f32(mine, masked, TN)
+        mine = dot(here8_bf, split_lanes(ratio), NN)
+        mine_hi = jnp.where(slot_row == SLOTS, 1.0, mine[:, :LANES])
+        mine2 = jnp.concatenate([mine_hi, mine[:, LANES:]], axis=0).astype(BF16)
+        weighted = raw * dot(mine2, masked2, TN)
         assign = weighted * (livef / jnp.sum(weighted, axis=0, keepdims=True))
 
         ah, al = split2(assign)
@@ -351,7 +390,7 @@
         for side, count_ in ((0, chips), (1, PAIRS - chips)):
             rows = pl.ds(side * chips * CHUNK, count_ * CHUNK)
             wide = dot(whi[rows, :], both, NT)
-            sums = wide[:, :LANES] + (wide[:, LANES:] + dot(wlo[rows, :], ah, NT))
+            sums = halves(wide) + dot(wlo[rows, :], ah, NT)
             sums = sums.reshape(count_, CHUNK, LANES) + chunk_name[None]
             s1[turn, pl.ds(side * chips, count_)] = sums
             c = lax.rem(core + side, 2)
@@ -394,9 +433,7 @@
                 goal = start + name
                 table = jnp.where(goal == iota(shape, 1).astype(F32), 1.0, 0.0)
                 e2[...] = table.astype(BF16)
-            hi, lo = split2(got)
-            table = e2[...]
-            part = dot(table, lo, TN) + dot(table, hi, TN)
+            part = halves(dot(e2[...], split_lanes(got), TN))
             s2[turn] = part.reshape(nx, dr, LANES)
 
             send = sender(sem + 4)
@@ -422,9 +459,7 @@
                 mean = jnp.sum(part * scale, axis=0, keepdims=True) / weight
                 betas.append((part - counts * mean) * scale)
             betas.append(whole[2 * SLIDES :])
-            hi, lo = split2(jnp.concatenate(betas, axis=0))
-            chosen = dot(e2[...], jnp.concatenate([hi, lo], axis=1), NN)
-            chosen = chosen[:, :LANES] + chosen[:, LANES:]
+            chosen = halves(dot(e2[...], split_lanes(jnp.concatenate(betas, axis=0)), NN))
             s4[turn] = chosen.reshape(ny, CHUNK, LANES)
 
             send = sender(sem + 6)
@@ -442,7 +477,8 @@
             arrivals(sem + 6, q4.at[turn, pl.ds(0, PAIRS * BACK)]).wait_recv()
 
         slot_beta = [q4[turn, pl.ds(i, ROWS, stride=5), :] for i in range(SLOTS)]
-        shifts = dot3(jnp.concatenate(slot_beta, axis=0), assign, NN)
+        bh, bl = split2(jnp.concatenate(slot_beta, axis=0))
+        shifts = dot(jnp.concatenate([bh, bh], axis=1), both, NN) + dot(bl, ah, NN)
         for i in range(SLOTS):
             field = field - shifts[i * ROWS : (i + 1) * ROWS] * masks[i]
         centre = q4[turn, pl.ds(SLOTS, ROWS, stride=5), :]
@@ -455,7 +491,7 @@
     for copy in pending:
         copy.wait_send()
     for turn in range(ITERS):
-        sem = turn * 7
+        sem = turn * 8
 
         @pl.when(pair < PAIRS)
         def _():
@@ -476,6 +512,9 @@
     vmem = pl.BlockSpec(memory_space=pltpu.VMEM)
     hbm = pl.BlockSpec(memory_space=pltpu.HBM)
 
+    def far(v):
+        return pltpu.with_memory_space_constraint(v, pltpu.HBM)
+
     def buf(*shape):
         return pltpu.VMEM((ITERS,) + shape, F32)
 
@@ -485,11 +524,13 @@
             jax.ShapeDtypeStruct(embedding.shape, F32),
             jax.ShapeDtypeStruct((PCS, CLUSTERS), F32),
         ),
-        in_specs=[hbm, hbm, vmem, vmem, vmem],
+        in_specs=[hbm, hbm, hbm, vmem, hbm],
         out_specs=(vmem, vmem),
         scratch_shapes=[
             pltpu.VMEM(embedding.shape, F32),
             pltpu.VMEM(neighbors.shape, jnp.int32),
+            pltpu.VMEM(slide_id.shape, jnp.int32),
+            pltpu.VMEM((PCS, CLUSTERS), F32),
             pltpu.VMEM((ROWS, cells + 8 * BOUND), F32),
             pltpu.VMEM((near, 8, cells), jnp.int32),
             pltpu.VMEM((cells + 8 * BOUND, cells), BF16),
@@ -501,10 +542,12 @@
             pltpu.VMEM((ny * CHUNK, LANES), BF16),
             buf(8, LANES),
             buf(nx, 8, LANES),
-            buf(SLIDES, LANES),
-            buf(len(NEAR) + 1, SLIDES, LANES),
-            buf(SLIDES, LANES),
-            buf(len(FAR) + 1, SLIDES, LANES),
+            buf(2, PADDED, LANES),
+            buf(PADDED, LANES),
+            buf(PADDED, LANES),
+            buf(SIDE * SIDE, PADDED, LANES),
+            buf(PADDED, LANES),
+            buf(2, PADDED, LANES),
             buf(PAIRS, CHUNK, LANES),
             buf(ny, CHUNK, LANES),
             buf(nx, dr, LANES),
@@ -513,18 +556,18 @@
             buf(nx, dr, LANES),
             buf(ny, CHUNK, LANES),
             buf(ROWS * 5 + 8, LANES),
-            pltpu.SemaphoreType.DMA((2,)),
+            pltpu.SemaphoreType.DMA((4,)),
             pltpu.SemaphoreType.DMA,
             pltpu.SemaphoreType.DMA,
-            pltpu.SemaphoreType.DMA((7 * ITERS,)),
-            pltpu.SemaphoreType.DMA((7 * ITERS,)),
+            pltpu.SemaphoreType.DMA((8 * ITERS,)),
+            pltpu.SemaphoreType.DMA((8 * ITERS,)),
             pltpu.SemaphoreType.REGULAR((6,)),
         ],
         compiler_params=pltpu.CompilerParams(
             collective_id=0, has_side_effects=True, vmem_limit_bytes=48 * 1024 * 1024
         ),
         name="harmony",
-    )(embedding, neighbors, slide_id, live_count, centroids.T)
+    )(far(embedding), far(neighbors), far(slide_id), live_count, far(centroids.T))
     return corrected, centers.T
 
 

time: 109 us -> 103 us (0.945)
  Pallas kernels: 104 us -> 100 us
  local copies, waits for them, and re-layouts: 3.66 us -> 1.25 us
    pallas_call x1, Pallas kernels: 104 us -> 100 us  [per_device(): pl.pallas_call(functools.partial(kernel, nx, ny), out_shape=(jax.ShapeDty...]
    unnamed x10 -> x2, local copies, waits for them, and re-layouts: 3.66 us -> 1.25 us
where the time goes in v3:
time: 103 us
  Pallas kernels  100 us (97%)
  between operations  1.29 us (1%)
  local copies, waits for them, and re-layouts  1.25 us (1%)
    pallas_call x1, Pallas kernels, per_device(): pl.pallas_call(functools.partial(kernel, nx, ny), out_shape=(jax.ShapeDty...  100 us

profile of v3, /device:TPU:1, one launch (start us, length us, event | category | flops | bytes accessed | tf_op | source)
XLA Modules:
  0.0 102.6 jit_solution(5183802013230822389)
XLA Ops:
  1.3 100.1 %harmony.1 = (f32[50,1,1,512]{3,2,1,0:T(1,128)S(1)}, f32[50,100]{1,0:T(8,128)S(1)}) custom-call(f32[50,1,1,512]{3,2,1,0:T(1,128)} %emb.1, s32[15,1,1,512]{3,2,1,0:T(1,128)} %nbr.1, s32[1,1,512]{2,1,0:T(1,128)} %sid.1, s32[1,1]{1,0:T(1,128)S(6)} %copy.9.live, f32[50,100]{1,0:T(8,128)} %bitcast.3), custom_call_target="tpu_custom_call" | custom-call | tf_op jit(solution)/shard_map/harmony/pallas_call | solution.py:521
  101.3 0.6 copy.10
  102.0 0.6 copy.11

commit v4 on v3

--- a/solution.py
+++ b/solution.py
@@ -130,7 +130,7 @@
         pl.semaphore_signal(sem, inc=1, device_id=tile(a, b), device_id_type=MESH)
 
     border = [(a, b) for a in (-1, 1) for b in (-1, 1)] + [(-1, 0), (1, 0), (0, -1), (0, 1)]
-    first_met = border + [(a, 0) for a in (-3, -2, 2, 3)]
+    first_met = border + [(a, 0) for a in (-4, -3, -2, 2, 3, 4)]
     for a, b in first_met:
         greet(bar, a, b)
 
@@ -174,7 +174,7 @@
         return c
 
     groups = cmat.shape[0] // 16
-    early = groups * 10 // 16
+    early = groups * 8 // 16
     lax.fori_loop(0, early, count, 0)
     get_emb.wait()
     own[:PCS, :cells] = embv[:, 0, 0, :]
@@ -199,8 +199,8 @@
         device_id_type=MESH,
     )
 
-    greet_tx(0, 3)
-    greet_ty(2, 1)
+    greet_tx(0, 4)
+    greet_ty(1, 1)
     lax.fori_loop(early, groups, count, 0)
 
     alive = iota((1, cells), 1) < live[...]
@@ -244,10 +244,8 @@
     cpad[:PCS, :CLUSTERS] = centv[...]
     centre = cpad[...]
 
-    heard(0)
-    greet_tx(1, 2)
-    heard(2)
-    greet_ty(3, 2)
+    heard(1)
+    greet_ty(2, 2)
     halo.wait_recv()
     everything = own[...]
     part1 = everything.astype(BF16).astype(F32)
@@ -259,9 +257,9 @@
     field = (everything[:, :cells] + summed) / (ids.shape[0] + 1.0)
     field = jnp.where(iota((ROWS, cells), 0) < PCS, field, 0.0) * livef
 
-    heard(3)
-    greet_ty(4, 4)
-    heard(1)
+    heard(2)
+    greet_ty(3, 4)
+    heard(0)
 
     cluster = iota((LANES, cells), 0)
     lane40 = iota((1, LANES), 1)
@@ -309,8 +307,8 @@
         r0[turn, 0, :SLOTS] = occ[:SLOTS]
 
         if turn == 0:
-            heard(4)
-            greet_ty(5, 8)
+            heard(3)
+            greet_ty(4, 8)
 
         slots_a = stack(by_slot + [(4, inverse)] + [(5 + i, masks[i]) for i in range(3)])
         slots_b = stack([(0, masks[3]), (1, inverse)])
@@ -330,7 +328,7 @@
         lax.fori_loop(0, PAIRS, build, 0)
 
         if turn == 0:
-            heard(5)
+            heard(4)
         copy = arrivals(sem, r0.at[turn, pl.ds(1, nx - 1), pl.ds(0, SLOTS)])
         copy.wait_recv()
         pending.append(copy)
@@ -505,6 +503,17 @@
             arrivals(sem + 3, q1.at[turn, pl.ds(0, PAIRS), pl.ds(0, SENT)]).wait_send()
 
 
+def hand_over(a, b, c, d, sems):
+    copies = [
+        pltpu.make_async_copy(a, c, sems.at[0]),
+        pltpu.make_async_copy(b, d, sems.at[1]),
+    ]
+    for copy in copies:
+        copy.start()
+    for copy in copies:
+        copy.wait()
+
+
 def per_device(nx, ny, embedding, neighbors, slide_id, live_count, centroids):
     cells = embedding.shape[3]
     near = neighbors.shape[0]
@@ -561,13 +570,27 @@
             pltpu.SemaphoreType.DMA,
             pltpu.SemaphoreType.DMA((8 * ITERS,)),
             pltpu.SemaphoreType.DMA((8 * ITERS,)),
-            pltpu.SemaphoreType.REGULAR((6,)),
+            pltpu.SemaphoreType.REGULAR((5,)),
         ],
         compiler_params=pltpu.CompilerParams(
             collective_id=0, has_side_effects=True, vmem_limit_bytes=48 * 1024 * 1024
         ),
         name="harmony",
     )(far(embedding), far(neighbors), far(slide_id), live_count, far(centroids.T))
+    corrected, centers = pl.pallas_call(
+        hand_over,
+        out_shape=(
+            jax.ShapeDtypeStruct(embedding.shape, F32),
+            jax.ShapeDtypeStruct((PCS, CLUSTERS), F32),
+        ),
+        in_specs=[vmem] * 2,
+        out_specs=(hbm, hbm),
+        scratch_shapes=[pltpu.SemaphoreType.DMA((2,))],
+        name="handover",
+    )(
+        pltpu.with_memory_space_constraint(corrected, pltpu.VMEM),
+        pltpu.with_memory_space_constraint(centers, pltpu.VMEM),
+    )
     return corrected, centers.T
 
 

time: 103 us -> 102 us (level)
  local copies, waits for them, and re-layouts: 1.25 us -> 0 us
    unnamed x2 -> x0, local copies, waits for them, and re-layouts: 1.25 us -> none
where the time goes in v4:
time: 102 us; the launch traced here: 101 us
  Pallas kernels  100 us (98%)
  between operations  1.28 us (1%)
    pallas_call x1, Pallas kernels, per_device(): pl.pallas_call(functools.partial(kernel, nx, ny), out_shape=(jax.ShapeDty...  99.5 us

profile of v4, /device:TPU:1, one launch (start us, length us, event | category | flops | bytes accessed | tf_op | source)
XLA Modules:
  0.0 101.5 jit_solution(7198051627853591157)
XLA Ops:
  1.3 99.5 %harmony.1 = (f32[50,1,1,512]{3,2,1,0:T(1,128)S(1)}, f32[50,100]{1,0:T(8,128)S(1)}) custom-call(f32[50,1,1,512]{3,2,1,0:T(1,128)} %emb.1, s32[15,1,1,512]{3,2,1,0:T(1,128)} %nbr.1, s32[1,1,512]{2,1,0:T(1,128)} %sid.1, s32[1,1]{1,0:T(1,128)S(6)} %copy.7.live, f32[50,100]{1,0:T(8,128)} %bitcast.2), custom_call_target="tpu_custom_call" | custom-call | tf_op jit(solution)/shard_map/harmony/pallas_call | solution.py:530
  100.8 0.7 handover.1

commit v5 on v4

--- a/solution.py
+++ b/solution.py
@@ -94,7 +94,7 @@
 def kernel(
     nx, ny, emb, nbr, sid, live, cent, out, outc,
     embv, nbrv, sidv, centv, own, nb, cmat, zs, whi, wlo, cpad, e0, e2,
-    f0, r0, f1, r1, f2, r2, f3, r3, s1, q1, s2, q2, s3, q3, s4, q4,
+    f0, r0, f2, r2, f3, r3, s1, q1, s2, q2, s3, q3, s4, q4,
     load, halo_s, halo_r, ss, rs, seen,
 ):
     cells = own.shape[1] - 8 * BOUND
@@ -130,7 +130,8 @@
         pl.semaphore_signal(sem, inc=1, device_id=tile(a, b), device_id_type=MESH)
 
     border = [(a, b) for a in (-1, 1) for b in (-1, 1)] + [(-1, 0), (1, 0), (0, -1), (0, 1)]
-    first_met = border + [(a, 0) for a in (-4, -3, -2, 2, 3, 4)]
+    other = 1 - 2 * core
+    first_met = border + [(a, b) for a in (-4, -3, -2, 2, 3, 4) for b in (0, other)]
     for a, b in first_met:
         greet(bar, a, b)
 
@@ -145,8 +146,7 @@
     def heard(step):
         pl.semaphore_wait(seen.at[step], 2)
 
-    r0[:, :, SLOTS:, :] = jnp.zeros((ITERS, nx, 8 - SLOTS, LANES), F32)
-    r1[:, HALF:, :] = jnp.zeros((ITERS, PADDED - HALF, LANES), F32)
+    r0[:, :, SLOTS:, :] = jnp.zeros((ITERS, 2 * nx, 8 - SLOTS, LANES), F32)
     r2[:, :, HALF:, :] = jnp.zeros((ITERS, SIDE * SIDE, PADDED - HALF, LANES), F32)
     r3[:, :, HALF:, :] = jnp.zeros((ITERS, 2, PADDED - HALF, LANES), F32)
     q1[:, :, SENT:, :] = jnp.zeros((ITERS, ny, CHUNK - SENT, LANES), F32)
@@ -302,8 +302,14 @@
 
         f0[turn] = occ
         send = sender(sem)
-        for r in across:
-            send(f0.at[turn, pl.ds(0, SLOTS)], r0.at[turn, r, pl.ds(0, SLOTS)], on_tx(r))
+        for r in across + [0]:
+            for c in (1, 0):
+                if r or c:
+                    send(
+                        f0.at[turn, pl.ds(0, SLOTS)],
+                        r0.at[turn, r * 2 + c, pl.ds(0, SLOTS)],
+                        (lax.rem(x + r, nx), chip * 2 + lax.rem(core + c, 2)),
+                    )
         r0[turn, 0, :SLOTS] = occ[:SLOTS]
 
         if turn == 0:
@@ -329,23 +335,16 @@
 
         if turn == 0:
             heard(4)
-        copy = arrivals(sem, r0.at[turn, pl.ds(1, nx - 1), pl.ds(0, SLOTS)])
+        copy = arrivals(sem, r0.at[turn, pl.ds(1, 2 * nx - 1), pl.ds(0, SLOTS)])
         copy.wait_recv()
         pending.append(copy)
-        got = r0[turn].reshape(nx * 8, LANES)
+        got = r0[turn].reshape(2 * nx * 8, LANES)
         if turn == 0:
-            name = jnp.broadcast_to(got[:, ID_LANE : ID_LANE + 1], (nx * 8, LANES))
-            lane = iota((nx * 8, LANES), 1).astype(F32)
-            slot = lax.rem(iota((nx * 8, LANES), 0), 8)
-            e0[...] = jnp.where((name == lane) & (slot < SLOTS), 1.0, 0.0).astype(BF16)
-        part = halves(dot(e0[...], split_lanes(got), TN)[: 2 * PADDED])
-        f1[turn] = part.reshape(2, PADDED, LANES)
-        send = sender(sem + 1)
-        send(f1.at[turn, 1 - core, pl.ds(0, HALF)], r1.at[turn, pl.ds(0, HALF)], on_ty(0, 0, 1))
-        copy = arrivals(sem + 1, r1.at[turn, pl.ds(0, HALF)])
-        copy.wait_recv()
-        pending.append(copy)
-        part = r1[turn] + f1[turn, core]
+            name = jnp.broadcast_to(got[:, ID_LANE : ID_LANE + 1], got.shape)
+            half_row = (iota(got.shape, 1) + core * PADDED).astype(F32)
+            slot = lax.rem(iota(got.shape, 0), 8)
+            e0[...] = jnp.where((name == half_row) & (slot < SLOTS), 1.0, 0.0).astype(BF16)
+        part = halves(dot(e0[...], split_lanes(got), TN)[:PADDED])
         f2[turn] = part
         send = sender(sem + 2)
         for a, b in SQUARE[:-1]:
@@ -457,16 +456,22 @@
                 mean = jnp.sum(part * scale, axis=0, keepdims=True) / weight
                 betas.append((part - counts * mean) * scale)
             betas.append(whole[2 * SLIDES :])
-            chosen = halves(dot(e2[...], split_lanes(jnp.concatenate(betas, axis=0)), NN))
-            s4[turn] = chosen.reshape(ny, CHUNK, LANES)
+            betas = split_lanes(jnp.concatenate(betas, axis=0))
 
             send = sender(sem + 6)
-            for a, b, c in OTHERS:
-                send(
-                    s4.at[turn, slot_of(a, b, c), pl.ds(0, BACK)],
-                    q4.at[turn, pl.ds(pair * BACK, BACK)],
-                    on_ty(SIDE - a, SIDE - b, 2 - c),
-                )
+            group = 2 * SIDE
+            for a in (2, 1, 3, 0):
+                rows = pl.ds(a * group * CHUNK, group * CHUNK)
+                chosen = halves(dot(e2[rows, :], betas, NN))
+                s4[turn, pl.ds(a * group, group)] = chosen.reshape(group, CHUNK, LANES)
+                for b in (2, 1, 3, 0):
+                    for c in (1, 0):
+                        if a or b or c:
+                            send(
+                                s4.at[turn, slot_of(a, b, c), pl.ds(0, BACK)],
+                                q4.at[turn, pl.ds(pair * BACK, BACK)],
+                                on_ty(SIDE - a, SIDE - b, 2 - c),
+                            )
             q4[turn, pl.ds(pair * BACK, BACK)] = s4[turn, 0, :BACK]
             arrivals(sem + 6, q4.at[turn, pl.ds(0, (PAIRS - 1) * BACK)]).wait_recv()
 
@@ -547,12 +552,10 @@
             pltpu.VMEM((PAIRS * CHUNK, cells), BF16),
             pltpu.VMEM((PAIRS * CHUNK, cells), BF16),
             pltpu.VMEM((ROWS, LANES), F32),
-            pltpu.VMEM((nx * 8, LANES), BF16),
+            pltpu.VMEM((2 * nx * 8, LANES), BF16),
             pltpu.VMEM((ny * CHUNK, LANES), BF16),
             buf(8, LANES),
-            buf(nx, 8, LANES),
-            buf(2, PADDED, LANES),
-            buf(PADDED, LANES),
+            buf(2 * nx, 8, LANES),
             buf(PADDED, LANES),
             buf(SIDE * SIDE, PADDED, LANES),
             buf(PADDED, LANES),

time: 102 us -> 100 us (0.980)
  Pallas kernels: 100 us -> 98.7 us
    pallas_call x1, Pallas kernels: 99.5 us -> 98.1 us  [per_device(): pl.pallas_call(functools.partial(kernel, nx, ny), out_shape=(jax.ShapeDty...]
where the time goes in v5:
time: 100 us
  Pallas kernels  98.7 us (99%)
  between operations  1.28 us (1%)
    pallas_call x1, Pallas kernels, per_device(): pl.pallas_call(functools.partial(kernel, nx, ny), out_shape=(jax.ShapeDty...  98.1 us

profile of v5, /device:TPU:1, one launch (start us, length us, event | category | flops | bytes accessed | tf_op | source)
XLA Modules:
  0.0 100.0 jit_solution(14639993499781490609)
XLA Ops:
  1.3 98.1 %harmony.1 = (f32[50,1,1,512]{3,2,1,0:T(1,128)S(1)}, f32[50,100]{1,0:T(8,128)S(1)}) custom-call(f32[50,1,1,512]{3,2,1,0:T(1,128)} %emb.1, s32[15,1,1,512]{3,2,1,0:T(1,128)} %nbr.1, s32[1,1,512]{2,1,0:T(1,128)} %sid.1, s32[1,1]{1,0:T(1,128)S(6)} %copy.7.live, f32[50,100]{1,0:T(8,128)} %bitcast.2), custom_call_target="tpu_custom_call" | custom-call | tf_op jit(solution)/shard_map/harmony/pallas_call | solution.py:535
  99.4 0.7 handover.1

commit v6 on v5

--- a/solution.py
+++ b/solution.py
@@ -93,7 +93,7 @@
 
 def kernel(
     nx, ny, emb, nbr, sid, live, cent, out, outc,
-    embv, nbrv, sidv, centv, own, nb, cmat, zs, whi, wlo, cpad, e0, e2,
+    embv, nbrv, sidv, centv, own, nb, cmat, zs, whi, wlo, cpad, e0, e2, e2t, n0, n1,
     f0, r0, f2, r2, f3, r3, s1, q1, s2, q2, s3, q3, s4, q4,
     load, halo_s, halo_r, ss, rs, seen,
 ):
@@ -233,13 +233,11 @@
     for i in range(SLOTS):
         name8 = jnp.where(slot_row == i, dense_row(names[i]), name8)
     here8_bf = jnp.where(slot_lane.astype(F32) == name8, 1.0, 0.0)[:, : 2 * PADDED].astype(BF16)
-    chunk_row = iota((CHUNK, LANES), 0)
-    chunk_lane = iota((CHUNK, LANES), 1)
-    chunk_name = jnp.zeros((CHUNK, LANES), F32)
-    for first in (0, 5, 10):
-        for i in range(SLOTS):
-            chunk_name = jnp.where(chunk_row == first + i, names[i], chunk_name)
-    chunk_name = jnp.where(chunk_lane == ID_LANE, chunk_name, 0.0)
+    own_name8 = jnp.full((8, LANES), NONE, F32)
+    for i in range(SLOTS):
+        own_name8 = jnp.where(slot_row == i, names[i], own_name8)
+    n0[...] = own_name8
+    n1[0] = own_name8
     get_cent.wait()
     cpad[:PCS, :CLUSTERS] = centv[...]
     centre = cpad[...]
@@ -335,6 +333,9 @@
 
         if turn == 0:
             heard(4)
+            send = sender(7 * ITERS + ITERS)
+            for offset in OTHERS:
+                send(n0.at[pl.ds(0, SLOTS)], n1.at[slot_of(*offset), pl.ds(0, SLOTS)], on_ty(*offset))
         copy = arrivals(sem, r0.at[turn, pl.ds(1, 2 * nx - 1), pl.ds(0, SLOTS)])
         copy.wait_recv()
         pending.append(copy)
@@ -354,6 +355,27 @@
                 on_ty(a, b, 0),
             )
         r2[turn, 0] = part
+        if turn == 0:
+            told = arrivals(7 * ITERS + ITERS, n1.at[pl.ds(1, ny - 1), pl.ds(0, SLOTS)])
+            told.wait_recv()
+            pending.append(told)
+            name4 = n1[:, :SLOTS, :]
+            gap = jnp.zeros((ny, 1, LANES), F32)
+            name = jnp.concatenate([name4, gap, name4, gap, name4, gap, gap], axis=1)
+            shape = (ny * CHUNK, LANES)
+            name = name.reshape(shape)
+            at = lax.rem(iota(shape, 0), CHUNK)
+            second = (at >= 5) & (at < 10)
+            middle = (at == 4) | (at == 9)
+            start = jnp.where(
+                middle,
+                3 * SLIDES + second.astype(jnp.int32),
+                jnp.where(second, SLIDES, jnp.where(at >= 10, 2 * SLIDES, 0)),
+            ).astype(F32)
+            goal = start + jnp.where(middle, 0.0, jnp.where(at < SENT, name, NONE))
+            table = jnp.where(goal == iota(shape, 1).astype(F32), 1.0, 0.0)
+            e2[...] = table.astype(BF16)
+            e2t[...] = table.T.astype(BF16)
         copy = arrivals(sem + 2, r2.at[turn, pl.ds(1, SIDE * SIDE - 1), pl.ds(0, HALF)])
         copy.wait_recv()
         pending.append(copy)
@@ -388,8 +410,7 @@
             rows = pl.ds(side * chips * CHUNK, count_ * CHUNK)
             wide = dot(whi[rows, :], both, NT)
             sums = halves(wide) + dot(wlo[rows, :], ah, NT)
-            sums = sums.reshape(count_, CHUNK, LANES) + chunk_name[None]
-            s1[turn, pl.ds(side * chips, count_)] = sums
+            s1[turn, pl.ds(side * chips, count_)] = sums.reshape(count_, CHUNK, LANES)
             c = lax.rem(core + side, 2)
             for a, b in SQUARE:
                 to = lax.rem(chip_y + a, SIDE) * SIDE + lax.rem(chip_x + b, SIDE)
@@ -415,22 +436,7 @@
             q1[turn, 0, :SENT] = s1[turn, pair, :SENT]
             arrivals(sem + 3, q1.at[turn, pl.ds(1, ny - 1), pl.ds(0, SENT)]).wait_recv()
             got = q1[turn].reshape(ny * CHUNK, LANES)
-            if turn == 0:
-                shape = (ny * CHUNK, LANES)
-                at = lax.rem(iota(shape, 0), CHUNK)
-                second = (at >= 5) & (at < 10)
-                middle = (at == 4) | (at == 9)
-                start = jnp.where(
-                    middle,
-                    3 * SLIDES + second.astype(jnp.int32),
-                    jnp.where(second, SLIDES, jnp.where(at >= 10, 2 * SLIDES, 0)),
-                ).astype(F32)
-                name = jnp.broadcast_to(got[:, ID_LANE : ID_LANE + 1], shape)
-                name = jnp.where(middle, 0.0, jnp.where(at < SENT, name, NONE))
-                goal = start + name
-                table = jnp.where(goal == iota(shape, 1).astype(F32), 1.0, 0.0)
-                e2[...] = table.astype(BF16)
-            part = halves(dot(e2[...], split_lanes(got), TN))
+            part = halves(dot(e2t[...], split_lanes(got), NN))
             s2[turn] = part.reshape(nx, dr, LANES)
 
             send = sender(sem + 4)
@@ -554,6 +560,9 @@
             pltpu.VMEM((ROWS, LANES), F32),
             pltpu.VMEM((2 * nx * 8, LANES), BF16),
             pltpu.VMEM((ny * CHUNK, LANES), BF16),
+            pltpu.VMEM((LANES, ny * CHUNK), BF16),
+            pltpu.VMEM((8, LANES), F32),
+            pltpu.VMEM((ny, 8, LANES), F32),
             buf(8, LANES),
             buf(2 * nx, 8, LANES),
             buf(PADDED, LANES),
@@ -571,8 +580,8 @@
             pltpu.SemaphoreType.DMA((4,)),
             pltpu.SemaphoreType.DMA,
             pltpu.SemaphoreType.DMA,
-            pltpu.SemaphoreType.DMA((8 * ITERS,)),
-            pltpu.SemaphoreType.DMA((8 * ITERS,)),
+            pltpu.SemaphoreType.DMA((8 * ITERS + 1,)),
+            pltpu.SemaphoreType.DMA((8 * ITERS + 1,)),
             pltpu.SemaphoreType.REGULAR((5,)),
         ],
         compiler_params=pltpu.CompilerParams(

time: 100 us -> 100 us (level)
  no operation moved by 1% of the time
where the time goes in v6:
time: 100 us
  Pallas kernels  98.7 us (99%)
  between operations  1.28 us (1%)
    pallas_call x1, Pallas kernels, per_device(): pl.pallas_call(functools.partial(kernel, nx, ny), out_shape=(jax.ShapeDty...  98 us

profile of v6, /device:TPU:1, one launch (start us, length us, event | category | flops | bytes accessed | tf_op | source)
XLA Modules:
  0.0 100.0 jit_solution(17660425401529370103)
XLA Ops:
  1.3 98.0 %harmony.1 = (f32[50,1,1,512]{3,2,1,0:T(1,128)S(1)}, f32[50,100]{1,0:T(8,128)S(1)}) custom-call(f32[50,1,1,512]{3,2,1,0:T(1,128)} %emb.1, s32[15,1,1,512]{3,2,1,0:T(1,128)} %nbr.1, s32[1,1,512]{2,1,0:T(1,128)} %sid.1, s32[1,1]{1,0:T(1,128)S(6)} %copy.7.live, f32[50,100]{1,0:T(8,128)} %bitcast.2), custom_call_target="tpu_custom_call" | custom-call | tf_op jit(solution)/shard_map/harmony/pallas_call | solution.py:541
  99.3 0.7 handover.1

commit v7 on v6

--- a/solution.py
+++ b/solution.py
@@ -255,8 +255,6 @@
     field = (everything[:, :cells] + summed) / (ids.shape[0] + 1.0)
     field = jnp.where(iota((ROWS, cells), 0) < PCS, field, 0.0) * livef
 
-    heard(2)
-    greet_ty(3, 4)
     heard(0)
 
     cluster = iota((LANES, cells), 0)
@@ -311,6 +309,8 @@
         r0[turn, 0, :SLOTS] = occ[:SLOTS]
 
         if turn == 0:
+            heard(2)
+            greet_ty(3, 4)
             heard(3)
             greet_ty(4, 8)
 

time: 100 us -> 100 us (level)
  no operation moved by 1% of the time
where the time goes in v7:
time: 100 us
  Pallas kernels  99 us (99%)
  between operations  1.28 us (1%)
    pallas_call x1, Pallas kernels, per_device(): pl.pallas_call(functools.partial(kernel, nx, ny), out_shape=(jax.ShapeDty...  98.4 us

profile of v7, /device:TPU:1, one launch (start us, length us, event | category | flops | bytes accessed | tf_op | source)
XLA Modules:
  0.0 100.3 jit_solution(16829449973410916937)
XLA Ops:
  1.3 98.4 %harmony.1 = (f32[50,1,1,512]{3,2,1,0:T(1,128)S(1)}, f32[50,100]{1,0:T(8,128)S(1)}) custom-call(f32[50,1,1,512]{3,2,1,0:T(1,128)} %emb.1, s32[15,1,1,512]{3,2,1,0:T(1,128)} %nbr.1, s32[1,1,512]{2,1,0:T(1,128)} %sid.1, s32[1,1]{1,0:T(1,128)S(6)} %copy.7.live, f32[50,100]{1,0:T(8,128)} %bitcast.2), custom_call_target="tpu_custom_call" | custom-call | tf_op jit(solution)/shard_map/harmony/pallas_call | solution.py:541
  99.7 0.7 handover.1
